TPU v7x, 128 devices: a whole 4x4x4 slice. The times are simulated.
128 devices in a mesh: axial: 16 (over x, y), azim: 8 (over z, core).
Axes of the slice: x: 4, y: 4, z: 4, core: 2. Of those that a mesh axis runs over, the one named last changes fastest.
Arguments:
- specific_heat_content: float32 [256, 1024, 512], P('axial', 'azim'), may hold values from -8 to 8
- phase: float32 [1024, 256, 256], P(('axial', 'azim')), may hold values from 0 to 1
- mobility: float32 [1024, 256, 256], P(('axial', 'azim')), may hold values from 0.5 to 2.4
- positions: int32 [1024, 3], replicated, may hold values from 0 to 1023, as said below
- counts: int32 [128], P(('axial', 'azim')), may hold values from 1 to 8, as said below
- neighbours: int32 [1024, 2], P(('axial', 'azim')), may hold values from 0 to 1023, as said below
Outputs:
- enthalpy_out: float32 [256, 1024, 512], P('axial', 'azim')
- phase_out: float32 [1024, 256, 256], P(('axial', 'azim'))
Inputs may be any that keep to these rules, and one draw needn't show every extreme that they name: `positions`: each patch lies at a cell of the grid, along each dimension within 0 to 255, 1023 and 511. `counts`: every device holds at least one live patch in its first slots; exactly one device holds 8. `neighbours`: for a live slot both entries are live slots of devices with the same azim index; in each azim index the live slots form one closed chain along the front through all of them. A slot that is not live names itself twice.
All inputs are finite; a program needn't handle non-finite values.
Results may differ from a plain program's by a relative error of at most 0.00002.
Values sent between devices are 32-bit elements; how exact they have to be, the bound alone decides.
A program may use at most 128 MiB of HBM per device.

v0:
```python
import jax
import jax.numpy as jnp
from jax import lax
from jax.sharding import PartitionSpec as P

PHASE_STEPS = 6


DT_MACRO = 0.1
DT_PHASE = 0.1
LATENT_HEAT = 1.0
DRIVE_GAIN = 2.0
COUPLING = 20.0


def extended(value, sides, width, wrap):
    for axis, dim in sides:
        size, length = (lax.axis_size(axis), value.shape[dim])
        up = [(i, (i + 1) % size) for i in range(size if wrap else size - 1)]
        down = [(j, i) for i, j in up]
        last = lax.slice_in_dim(value, length - width, length, axis=dim)
        initial = lax.slice_in_dim(value, 0, width, axis=dim)
        before = lax.ppermute(last, axis, up)
        after = lax.ppermute(initial, axis, down)
        value = jnp.concatenate([before, value, after], axis=dim)
    return value


def thermal_distribution(quantity_lines):
    return jnp.minimum(quantity_lines, 0.0) + jnp.maximum(quantity_lines - LATENT_HEAT, 0.0)


def advance(current, mobility, drive, column_pad):
    solid_row = jnp.ones_like(current[:, :1, :])
    liquid_row = jnp.zeros_like(current[:, :1, :])
    row_pad = jnp.concatenate([solid_row, current, liquid_row], axis=1)
    diffusion_operator = (
        row_pad[:, :-2]
        + row_pad[:, 2:]
        + column_pad[:, :, :-2]
        + column_pad[:, :, 2:]
        - 4.0 * current
    )
    reaction = current * (1.0 - current) * (current - 0.5 - DRIVE_GAIN * drive)
    return current + DT_PHASE * mobility * (diffusion_operator + reaction)


def shards(specific_heat_content, phase, mobility, positions, counts, neighbours):
    thermal_lines = thermal_distribution(specific_heat_content)
    lengthwise_margin = extended(thermal_lines, (("axial", 0),), 1, False)
    angular_margin = extended(thermal_lines, (("azim", 1),), 1, True)
    spoke_margin = jnp.pad(thermal_lines, ((0, 0), (0, 0), (1, 1)))
    diffusion_operator = (
        lengthwise_margin[2:]
        + lengthwise_margin[:-2]
        + angular_margin[:, 2:]
        + angular_margin[:, :-2]
        + spoke_margin[:, :, 2:]
        + spoke_margin[:, :, :-2]
        - 6.0 * thermal_lines
    )
    warmed_snapshot = specific_heat_content + DT_MACRO * diffusion_operator
    chilled_snapshot = thermal_distribution(warmed_snapshot)
    cells_x, cells_y, cells_z = specific_heat_content.shape
    local_x = positions[:, 0] - lax.axis_index("axial") * cells_x
    local_y = positions[:, 1] - lax.axis_index("azim") * cells_y
    inside = (local_x >= 0) & (local_x < cells_x) & (local_y >= 0) & (local_y < cells_y)
    flat_index = (
        jnp.clip(local_x, 0, cells_x - 1) * (cells_y * cells_z)
        + jnp.clip(local_y, 0, cells_y - 1) * cells_z
        + positions[:, 2]
    )
    sampled = jnp.where(inside, chilled_snapshot.reshape(-1)[flat_index], 0.0)
    patch_temps = lax.psum_scatter(sampled, ("axial", "azim"), scatter_dimension=0, tiled=True)
    capacity = phase.shape[0]
    live_slots = jnp.arange(capacity, dtype=jnp.int32) < counts[0]
    azim_count = lax.axis_size("azim")
    prev_rows = neighbours[:, 0] // capacity // azim_count * capacity + neighbours[:, 0] % capacity
    next_rows = neighbours[:, 1] // capacity // azim_count * capacity + neighbours[:, 1] % capacity
    drive = patch_temps[:, None, None]
    current = phase
    for iteration in range(PHASE_STEPS):
        edges = jnp.stack([current[:, :, 0], current[:, :, -1]], axis=1)
        gathered = lax.all_gather(edges, "axial", axis=0, tiled=True)
        left_edge = gathered[prev_rows, 1]
        right_edge = gathered[next_rows, 0]
        column_pad = jnp.concatenate(
            [left_edge[:, :, None], current, right_edge[:, :, None]], axis=2
        )
        current = advance(current, mobility, drive, column_pad)
    latent = jnp.where(live_slots, COUPLING * jnp.mean(current - phase, axis=(1, 2)), 0.0)
    phase_out = jnp.where(live_slots[:, None, None], current, phase)
    all_latent = lax.all_gather(latent, ("axial", "azim"), axis=0, tiled=True)
    released = jnp.where(inside, all_latent, 0.0)
    enthalpy_out = (
        warmed_snapshot.reshape(-1)
        .at[flat_index]
        .add(released)
        .reshape(specific_heat_content.shape)
    )
    return (enthalpy_out, phase_out)


def solution(mesh):
    in_specs = (
        P("axial", "azim", None),
        P(("axial", "azim"), None, None),
        P(("axial", "azim"), None, None),
        P(),
        P(("axial", "azim")),
        P(("axial", "azim"), None),
    )
    out_specs = (P("axial", "azim", None), P(("axial", "azim"), None, None))
    return jax.shard_map(shards, mesh=mesh, in_specs=in_specs, out_specs=out_specs, check_vma=False)
```

profile of v0, /device:TPU:1, one launch (start us, length us, event | category | flops | bytes accessed | tf_op | source)
XLA Modules:
  0.0 417.3 jit_solution(4754109502186849164)
XLA Ops:
  0.6 2.9 maximum_add_fusion.1
  3.6 1.3 collective-permute-start
  4.9 4.7 %collective-permute-start.1 = (f32[1,128,512]{2,1,0:T(8,128)S(1)}, f32[1,128,512]{2,1,0:T(8,128)S(1)}, u32[]{:S(2)}, u32[]{:S(2)}) collective-permute-start(f32[1,128,512]{2,1,0:T(8,128)S(1)} %get-tuple-element.13), channel_id=1, source_target_pairs={{0,8},{8,16},{16,24},{24,32},{32,40},{40,48},{48,56},{56,64},{64,7... | collective-permute-start | bytes 786440 | tf_op jit(solution)/shard_map/ppermute | solution.py:23
  9.6 0.6 fusion.68
  10.2 1.3 collective-permute-start.2
  11.5 1.6 collective-permute-start.3
  13.3 1.9 copy.57
  16.0 21.3 %all_gather.21 = f32[128,2,256]{2,1,0:T(2,128)S(1)} all-gather(f32[8,2,256]{2,1,0:T(2,128)S(1)} %pad_maximum_fusion.16), channel_id=1, replica_groups=mesh['axial'=16,'azim'=8] {'axial'}, dimensions={0}, use_global_device_ids=true | all-gather | bytes 278528 | tf_op jit(solution)/shard_map/all_gather | solution.py:84
  37.3 0.6 gather_fusion
  37.9 0.6 gather_fusion.1
  38.5 1.9 copy.44
  40.5 17.2 %maximum_add_fusion = (f32[16,128,512]{2,1,0:T(8,128)S(1)}, f32[16,128,512]{2,1,0:T(8,128)}) fusion(f32[16,128,512]{2,1,0:T(8,128)} %param.6, f32[16,128,512]{2,1,0:T(8,128)} %copy-done.2, f32[16,1,512]{2,1,0:T(1,128)S(1)} %collective-permute-done.3, f32[16,1,512]{2,1,0:T(1,128)S(1)} %collective-permute-done.2, ...), kind=kLoop, calls=%fused_computation.28 | loop fusion | flops 17825792 | bytes 17367040 | tf_op jit(solution)/shard_map/add | solution.py:30
  57.6 3.1 copy.72
  60.7 35.0 %gather_fusion.2 = f32[1024]{0:T(1024)S(1)} fusion(f32[1048576]{0:T(1024)} %bitcast.49, s32[1024]{0:T(1024)S(1)} %broadcast_clamp_fusion), kind=kCustom, calls=%fused_computation.2 | custom fusion | bytes 12288 | tf_op jit(solution)/shard_map/gather | solution.py:73
  95.7 72.2 %all-reduce.16 = f32[1024]{0:T(1024)S(1)} all-reduce(f32[1024]{0:T(1024)S(1)} %broadcast_select_fusion.2), channel_id=2, replica_groups=mesh['axial'=16,'azim'=8] {'axial','azim'}, use_global_device_ids=true, to_apply=%region_0.1.clone | all-reduce | flops 1024 | bytes 8192
  168.0 6.5 %fusion.14 = f32[8,256,256]{1,2,0:T(8,128)S(1)} fusion(f32[8,256,256]{1,2,0:T(8,128)} %copy-done, f32[8,256,1]{1,2,0:T(1,128)S(1)} %copy.52, f32[8,256,1]{1,2,0:T(1,128)S(1)} %copy.49, f32[8,256,256]{1,2,0:T(8,128)S(1)} %copy.44, f32[8]{0:T(128)S(1)} %dynamic-slice_multiply_fusion), kind=kLoop, calls=%fused_computation.54 | loop fusion | flops 8388608 | bytes 6307872 | tf_op jit(solution)/shard_map/add | solution.py:45
  174.6 1.3 copy-done.6
  175.9 16.3 %all_gather.22 = f32[128,2,256]{2,1,0:T(2,128)S(1)} all-gather(f32[8,2,256]{2,1,0:T(2,128)S(1)} %pad_maximum_fusion.17), channel_id=1, replica_groups=mesh['axial'=16,'azim'=8] {'axial'}, dimensions={0}, use_global_device_ids=true | all-gather | bytes 278528 | tf_op jit(solution)/shard_map/all_gather | solution.py:84
  192.2 0.6 gather_fusion.3
  192.8 0.6 gather_fusion.4
  193.4 6.5 %fusion.22 = f32[8,256,256]{1,2,0:T(8,128)S(1)} fusion(f32[8,256,256]{1,2,0:T(8,128)} %copy-done.6, f32[8,256,1]{1,2,0:T(1,128)S(1)} %copy.59, f32[8,256,1]{1,2,0:T(1,128)S(1)} %copy.58, f32[8,256,256]{1,2,0:T(8,128)S(1)} %copy.44, f32[8]{0:T(128)S(1)} %dynamic-slice_multiply_fusion), kind=kLoop, calls=%fused_computation.62 | loop fusion | flops 8388608 | bytes 6307872 | tf_op jit(solution)/shard_map/add | solution.py:45
  199.9 1.3 copy-done.3
  201.3 17.6 %all_gather.23 = f32[128,2,256]{2,1,0:T(2,128)S(1)} all-gather(f32[8,2,256]{2,1,0:T(2,128)S(1)} %pad_maximum_fusion.18), channel_id=1, replica_groups=mesh['axial'=16,'azim'=8] {'axial'}, dimensions={0}, use_global_device_ids=true | all-gather | bytes 278528 | tf_op jit(solution)/shard_map/all_gather | solution.py:84
  218.9 0.6 gather_fusion.5
  219.5 0.6 gather_fusion.6
  220.1 6.5 %fusion.30 = f32[8,256,256]{1,2,0:T(8,128)S(1)} fusion(f32[8,256,256]{1,2,0:T(8,128)} %copy-done.3, f32[8,256,1]{1,2,0:T(1,128)S(1)} %copy.61, f32[8,256,1]{1,2,0:T(1,128)S(1)} %copy.60, f32[8,256,256]{1,2,0:T(8,128)S(1)} %copy.44, f32[8]{0:T(128)S(1)} %dynamic-slice_multiply_fusion), kind=kLoop, calls=%fused_computation.70 | loop fusion | flops 8388608 | bytes 6307872 | tf_op jit(solution)/shard_map/add | solution.py:45
  226.6 1.3 copy-done.4
  227.9 16.2 %all_gather.24 = f32[128,2,256]{2,1,0:T(2,128)S(1)} all-gather(f32[8,2,256]{2,1,0:T(2,128)S(1)} %pad_maximum_fusion.19), channel_id=1, replica_groups=mesh['axial'=16,'azim'=8] {'axial'}, dimensions={0}, use_global_device_ids=true | all-gather | bytes 278528 | tf_op jit(solution)/shard_map/all_gather | solution.py:84
  244.1 0.6 gather_fusion.7
  244.7 0.6 gather_fusion.8
  245.3 6.5 %fusion.38 = f32[8,256,256]{1,2,0:T(8,128)S(1)} fusion(f32[8,256,256]{1,2,0:T(8,128)} %copy-done.4, f32[8,256,1]{1,2,0:T(1,128)S(1)} %copy.63, f32[8,256,1]{1,2,0:T(1,128)S(1)} %copy.62, f32[8,256,256]{1,2,0:T(8,128)S(1)} %copy.44, f32[8]{0:T(128)S(1)} %dynamic-slice_multiply_fusion), kind=kLoop, calls=%fused_computation.78 | loop fusion | flops 8388608 | bytes 6307872 | tf_op jit(solution)/shard_map/add | solution.py:45
  251.8 1.3 copy-done.5
  253.1 17.6 %all_gather.25 = f32[128,2,256]{2,1,0:T(2,128)S(1)} all-gather(f32[8,2,256]{2,1,0:T(2,128)S(1)} %pad_maximum_fusion.20), channel_id=1, replica_groups=mesh['axial'=16,'azim'=8] {'axial'}, dimensions={0}, use_global_device_ids=true | all-gather | bytes 278528 | tf_op jit(solution)/shard_map/all_gather | solution.py:84
  270.8 0.6 gather_fusion.9
  271.4 0.6 gather_fusion.10
  272.0 6.5 %fusion.46 = f32[8,256,256]{1,2,0:T(8,128)S(1)} fusion(f32[8,256,256]{1,2,0:T(8,128)} %copy-done.5, f32[8,256,1]{1,2,0:T(1,128)S(1)} %copy.65, f32[8,256,1]{1,2,0:T(1,128)S(1)} %copy.64, f32[8,256,256]{1,2,0:T(8,128)S(1)} %copy.44, f32[8]{0:T(128)S(1)} %dynamic-slice_multiply_fusion), kind=kLoop, calls=%fused_computation.86 | loop fusion | flops 8388608 | bytes 6307872 | tf_op jit(solution)/shard_map/add | solution.py:45
  278.5 1.3 copy-done.7
  279.8 16.3 %all_gather.26 = f32[128,2,256]{2,1,0:T(2,128)S(1)} all-gather(f32[8,2,256]{2,1,0:T(2,128)S(1)} %pad_maximum_fusion.21), channel_id=1, replica_groups=mesh['axial'=16,'azim'=8] {'axial'}, dimensions={0}, use_global_device_ids=true | all-gather | bytes 278528 | tf_op jit(solution)/shard_map/all_gather | solution.py:84
  296.1 0.6 gather_fusion.11
  296.7 0.6 gather_fusion.12
  297.3 8.0 %broadcast_select_fusion = (f32[8,256,256]{1,2,0:T(8,128)}, f32[8,256,256]{1,2,0:T(8,128)S(1)}) fusion(f32[8,256,256]{1,2,0:T(8,128)} %copy-done, pred[8]{0:T(512)(128)(4,1)S(1)} %iota_compare_fusion, f32[8,256,256]{1,2,0:T(8,128)} %copy-done.7, f32[8]{0:T(128)S(1)} %dynamic-slice_multiply_fusion, f32[8,256,1]{1,2,0:T(1,128)S(1)} %copy.67, ...), kind=kLoop, calls=%fused_computation.109 | loop fusion | flops 8912896 | bytes 10502184 | tf_op jit(solution)/shard_map/jit(_where)/select_n | solution.py:92
  305.3 0.5 subtract_reduce_fusion
  305.8 0.1 select_dynamic-update-slice_fusion
  305.9 89.2 %all-reduce.15 = f32[1024]{0:T(1024)S(1)} all-reduce(f32[1024]{0:T(1024)S(1)} %select_dynamic-update-slice_fusion), channel_id=1, replica_groups=mesh['axial'=16,'azim'=8] {'axial','azim'}, use_global_device_ids=true, to_apply=%add.15 | all-reduce | flops 1024 | bytes 8192
  395.1 5.2 %copy.71 = f32[256,4,8,128]{3,1,2,0:T(4,128)} copy(f32[256,4,8,128]{3,2,1,0:T(8,128)} %bitcast.50) | data formatting | bytes 8388608
  400.4 10.0 %scatter_fusion = f32[1048576]{0:T(1024)} fusion(f32[1048576]{0:T(1024)} %bitcast.48, s32[1024]{0:T(1024)S(1)} %bitcast.53, f32[1024]{0:T(1024)S(1)} %broadcast_select_fusion.1), kind=kCustom, calls=%fused_computation.13 | custom fusion | flops 1024 | bytes 16384 | tf_op jit(solution)/shard_map/scatter-add | solution.py:98
  410.4 5.1 %reshape.35 = f32[16,128,512]{2,1,0:T(8,128)} reshape(f32[1048576]{0:T(1024)} %scatter_fusion) | data formatting | bytes 8388608 | tf_op jit(solution)/shard_map/reshape | solution.py:99
  415.4 1.8 copy.70
  (55 shorter events, 0.6 us)
Async XLA Ops:
  0.6 12.5 %copy-start.9 = (s32[1024,3]{0,1:T(4,128)S(1)}, s32[1024,3]{0,1:T(4,128)}, u32[]{:S(2)}) copy-start(s32[1024,3]{0,1:T(4,128)} %param.9) | copy-start | bytes 36868
  3.5 6.0 %copy-start.2 = (f32[16,128,512]{2,1,0:T(8,128)}, f32[16,128,512]{2,1,0:T(8,128)S(1)}, u32[]{:S(2)}) copy-start(f32[16,128,512]{2,1,0:T(8,128)S(1)} %maximum_add_fusion.1) | copy-start | bytes 12582916
  3.6 36.8 %collective-permute-start = (f32[1,128,512]{2,1,0:T(8,128)S(1)}, f32[1,128,512]{2,1,0:T(8,128)S(1)}, u32[]{:S(2)}, u32[]{:S(2)}) collective-permute-start(f32[1,128,512]{2,1,0:T(8,128)S(1)} %get-tuple-element.12), channel_id=1, source_target_pairs={{8,0},{16,8},{24,16},{32,24},{40,32},{48,40},{56,48},{64,56},{72,6... | collective-permute-start | bytes 786440 | tf_op jit(solution)/shard_map/ppermute | solution.py:24
  4.9 35.6 %collective-permute-start.1 = (f32[1,128,512]{2,1,0:T(8,128)S(1)}, f32[1,128,512]{2,1,0:T(8,128)S(1)}, u32[]{:S(2)}, u32[]{:S(2)}) collective-permute-start(f32[1,128,512]{2,1,0:T(8,128)S(1)} %get-tuple-element.13), channel_id=1, source_target_pairs={{0,8},{8,16},{16,24},{24,32},{32,40},{40,48},{48,56},{56,64},{64,7... | collective-permute-start | bytes 786440 | tf_op jit(solution)/shard_map/ppermute | solution.py:23
  10.2 30.2 %collective-permute-start.2 = (f32[16,1,512]{2,1,0:T(1,128)}, f32[16,1,512]{2,1,0:T(1,128)S(1)}, u32[]{:S(2)}, u32[]{:S(2)}) collective-permute-start(f32[16,1,512]{2,1,0:T(1,128)} %get-tuple-element.14), channel_id=1, source_target_pairs={{1,0},{2,1},{3,2},{4,3},{5,4},{6,5},{7,6},{0,7},{9,8},{10,9},{11,1... | collective-permute-start | bytes 98312 | tf_op jit(solution)/shard_map/ppermute | solution.py:24
  11.5 28.9 %collective-permute-start.3 = (f32[16,1,512]{2,1,0:T(1,128)S(1)}, f32[16,1,512]{2,1,0:T(1,128)S(1)}, u32[]{:S(2)}, u32[]{:S(2)}) collective-permute-start(f32[16,1,512]{2,1,0:T(1,128)S(1)} %get-tuple-element.15), channel_id=1, source_target_pairs={{0,1},{1,2},{2,3},{3,4},{4,5},{5,6},{6,7},{7,0},{8,9},{9,10},{10,1... | collective-permute-start | bytes 98312 | tf_op jit(solution)/shard_map/ppermute | solution.py:23
  13.2 2.7 copy-start.10
  15.2 23.2 %copy-start = (f32[8,256,256]{1,2,0:T(8,128)}, f32[8,256,256]{1,2,0:T(8,128)S(1)}, u32[]{:S(2)}) copy-start(f32[8,256,256]{1,2,0:T(8,128)S(1)} %copy.57) | copy-start | bytes 6291460
  174.6 1.3 copy-start.6
  199.9 1.3 copy-start.3
  226.6 1.3 copy-start.4
  251.8 1.3 copy-start.5
  278.5 1.3 copy-start.7
  297.3 8.0 %copy-start.1 = (f32[8,256,256]{1,2,0:T(8,128)S(1)}, f32[8,256,256]{1,2,0:T(8,128)}, u32[]{:S(2)}) copy-start(f32[8,256,256]{1,2,0:T(8,128)} %copy-done) | copy-start | bytes 6291460
  410.4 5.1 %copy-start.8 = (f32[8,256,256]{1,2,0:T(8,128)S(1)}, f32[8,256,256]{1,2,0:T(8,128)}, u32[]{:S(2)}) copy-start(f32[8,256,256]{1,2,0:T(8,128)} %get-tuple-element.8) | copy-start | bytes 6291460
where the time goes:
time: 419 us; the launch traced here: 417 us
  blocking collectives  267 us (64%)
  other arithmetic  71.4 us (17%)
  local copies, waits for them, and re-layouts  68.5 us (16%)
  starting transfers between devices  8.88 us (2%)
    unnamed x2, blocking collectives  161 us
    all_gather x6, blocking collectives, shards(): gathered = lax.all_gather(edges, 'axial', axis=0, tiled=True)  105 us
    gather x1, local copies, waits for them, and re-layouts, shards(): sampled = jnp.where(inside, chilled_snapshot.reshape(-1)[flat_index], 0.0)  35 us
    add x5, other arithmetic, advance(): return current + DT_PHASE * mobility * (diffusion_operator + reaction)  32.4 us
    unnamed x28, local copies, waits for them, and re-layouts  20.6 us
    add x2, other arithmetic, thermal_distribution(): jnp.minimum(quantity_lines, 0.0)  20.1 us
    scatter-add x1, other arithmetic, shards(): enthalpy_out = warmed_snapshot.reshape(-1).at[flat_index].add(released).r...  10 us
  transfers between devices with their start and end apart: 4, of which 0 were waited for; matrix products, arithmetic and copies ran while one was open for 1% of the time, Pallas kernels for 0%

commit v1 on v0

--- a/solution.py
+++ b/solution.py
@@ -1,16 +1,30 @@
 import jax
 import jax.numpy as jnp
 from jax import lax
+from jax.experimental import pallas as pl
+from jax.experimental.pallas import tpu as pltpu
 from jax.sharding import PartitionSpec as P
 
 PHASE_STEPS = 6
-
-
 DT_MACRO = 0.1
 DT_PHASE = 0.1
 LATENT_HEAT = 1.0
 DRIVE_GAIN = 2.0
 COUPLING = 20.0
+
+NA = 16
+NB = 8
+SLOTS = 8
+SIDE = 256
+CX, CY, CZ = 16, 128, 512
+CAP = 6
+EDGE_ROWS = 24
+MESH = pl.DeviceIdType.MESH
+F32 = jnp.float32
+I32 = jnp.int32
+VMEM = pltpu.VMEM
+SMEM = pltpu.SMEM
+DMA = pltpu.SemaphoreType.DMA
 
 
 def extended(value, sides, width, wrap):
@@ -45,7 +59,7 @@
     return current + DT_PHASE * mobility * (diffusion_operator + reaction)
 
 
-def shards(specific_heat_content, phase, mobility, positions, counts, neighbours):
+def general(specific_heat_content, phase, mobility, positions, counts, neighbours):
     thermal_lines = thermal_distribution(specific_heat_content)
     lengthwise_margin = extended(thermal_lines, (("axial", 0),), 1, False)
     angular_margin = extended(thermal_lines, (("azim", 1),), 1, True)
@@ -101,6 +115,473 @@
     return (enthalpy_out, phase_out)
 
 
+def local_cell(x, y, a, b):
+    return x - a * CX, ((y - b * CY + 1) & (NB * CY - 1)) - 1
+
+
+def sample_kernel(pos_ref, spos_ref, e_hbm, c_ref, hits_ref, e_ref, sem):
+    load = pltpu.make_async_copy(e_hbm, e_ref, sem)
+    load.start()
+    a, b = lax.axis_index("axial"), lax.axis_index("azim")
+    lx, ly = local_cell(pos_ref[0], pos_ref[1], a, b)
+    inx = (lx >= 0) & (lx < CX)
+    iny = (ly >= 0) & (ly < CY)
+    touched = (inx & (ly <= CY)) | (iny & (lx >= -1) & (lx <= CX))
+    mark = jnp.where(touched, 1.0, 0.0).astype(F32)
+    row = lax.broadcasted_iota(I32, (128, 128), 0)
+    col = lax.broadcasted_iota(I32, (128, 128), 1)
+    before = jnp.where(row < col, 1.0, 0.0).astype(F32)
+    within = jnp.dot(mark, before, preferred_element_type=F32)
+    totals = jnp.dot(mark, jnp.ones((128, 128), F32), preferred_element_type=F32)
+    row8 = lax.broadcasted_iota(I32, (8, 8), 0)
+    col8 = lax.broadcasted_iota(I32, (8, 8), 1)
+    above = jnp.dot(jnp.where(col8 < row8, 1.0, 0.0).astype(F32), totals, preferred_element_type=F32)
+    rank = jnp.where(touched, within + above, -1.0)
+    linear = lax.broadcasted_iota(I32, (8, 128), 0) * 128 + lax.broadcasted_iota(I32, (8, 128), 1)
+    count = jnp.sum(mark).astype(I32)
+    hits_ref[0] = count
+    c_ref[...] = jnp.zeros((8, 128), F32)
+    lane = lax.broadcasted_iota(I32, (1, CZ), 1)
+    load.wait()
+    group = 4
+
+    def chunk(i, carry):
+        acc = c_ref[...]
+        for j in range(group):
+            h = i * group + j
+            s = jnp.sum(jnp.where(rank == h.astype(F32), linear, 0))
+            hits_ref[h + 1] = s
+            valid = h < count
+            px, py = local_cell(spos_ref[s], spos_ref[NA * NB * SLOTS + s], a, b)
+            z = spos_ref[2 * NA * NB * SLOTS + s]
+            okx = (px >= 0) & (px < CX) & valid
+            oky = (py >= 0) & (py < CY) & valid
+            x0 = jnp.clip(px, 0, CX - 1)
+            y0 = jnp.clip(py, 0, CY - 1)
+
+            def part(x, y, ok):
+                t = thermal_distribution(e_ref[jnp.clip(x, 0, CX - 1), pl.ds(jnp.clip(y, 0, CY - 1), 1), :])
+                return jnp.where(ok, t, 0.0)
+
+            inside = okx & oky
+            own = jnp.where(inside, e_ref[x0, pl.ds(y0, 1), :], 0.0)
+            t = thermal_distribution(own)
+            ring = (
+                part(px - 1, y0, oky & (px >= 1) & (px <= CX))
+                + part(px + 1, y0, oky & (px >= -1) & (px < CX - 1))
+                + part(x0, py - 1, okx & (py >= 1) & (py <= CY))
+                + part(x0, py + 1, okx & (py >= -1) & (py < CY - 1))
+            )
+            here = lane == z
+            beside = (lane == z - 1) | (lane == z + 1)
+            value = jnp.where(here, own + DT_MACRO * (ring - 6.0 * t), 0.0) + jnp.where(beside, DT_MACRO * t, 0.0)
+            acc = acc + jnp.where((linear == s) & valid, jnp.sum(value, keepdims=True), 0.0)
+        c_ref[...] = acc
+        return carry
+
+    lax.fori_loop(0, (count + group - 1) // group, chunk, 0)
+
+
+def lane_sum(halves, lane):
+    first, second = halves
+    l0, l1 = pltpu.roll(first, 1, 1), pltpu.roll(second, 1, 1)
+    r0, r1 = pltpu.roll(first, 127, 1), pltpu.roll(second, 127, 1)
+    low, high = lane == 0, lane == 127
+    return (
+        jnp.where(low, 1.0, l0) + jnp.where(high, r1, r0),
+        jnp.where(low, l0, l1) + jnp.where(high, 0.0, r1),
+    )
+
+
+def phase_step(halves, rates, k1, k4, lane):
+    rows = halves[0].shape[0]
+    beside = lane_sum(halves, lane)
+    out = []
+    for h in range(2):
+        c = halves[h]
+        around = beside[h] + (pltpu.roll(c, 1, 0) + pltpu.roll(c, rows - 1, 0))
+        out.append(c + rates[h] * (around + c * (c * (k1 - c) - k4)))
+    return tuple(out)
+
+
+def main_kernel(
+    send_ref, recv_ref, place_ref, c_ref, flag_ref, live_ref, e_hbm, phase_hbm, mob_hbm,
+    heated_ref, out_ref, latent_ref, over_ref,
+    e_ref, t_ref, p_ref, m_ref, pt, mt, ct, eb, sb, rb, stp, stm,
+    hx, hy, ty, c_out, c1, c2, sum1, lat, l1, l2, latsum, nb_t,
+    load_sem, s1s, s1r, s2s, s2r, es, er, hxs, hxr, hys, hyr, l1s, l1r, l2s, l2r,
+):
+    a, b = lax.axis_index("axial"), lax.axis_index("azim")
+    ax = [(lax.rem(a + i, NA), b) for i in range(1, NA)]
+    az = [(a, lax.rem(b + i, NB)) for i in range(1, NB)]
+    barrier = pltpu.get_barrier_semaphore()
+    for peer in az + ax:
+        pl.semaphore_signal(barrier, inc=1, device_id=peer, device_id_type=MESH)
+
+    load_p = pltpu.make_async_copy(phase_hbm, p_ref, load_sem.at[0])
+    load_m = pltpu.make_async_copy(mob_hbm, m_ref, load_sem.at[1])
+    load_e = pltpu.make_async_copy(e_hbm, e_ref, load_sem.at[2])
+    load_p.start()
+    load_m.start()
+    load_e.start()
+    for j in range(NB):
+        c_out[j, 0:1, :] = c_ref[j : j + 1, :]
+        c_out[j, 1:2, :] = flag_ref[...]
+    load_p.wait()
+    load_m.wait()
+
+    @pl.loop(0, SLOTS)
+    def _(s):
+        p = p_ref[s].T
+        m = m_ref[s].T * DT_PHASE
+        for h in range(2):
+            ph, mh = p[:, h * 128 : h * 128 + 128], m[:, h * 128 : h * 128 + 128]
+            pt[s, h] = ph
+            mt[s, h] = mh
+            base = h * 12
+            eb[2 * s, base : base + 6] = ph[0:6]
+            eb[2 * s, base + 6 : base + 11] = mh[0:5]
+            eb[2 * s + 1, base : base + 6] = ph[250:256]
+            eb[2 * s + 1, base + 6 : base + 11] = mh[251:256]
+            eb[2 * s, base + 11 : base + 12] = jnp.zeros((1, 128), F32)
+            eb[2 * s + 1, base + 11 : base + 12] = jnp.zeros((1, 128), F32)
+
+    pl.semaphore_wait(barrier, len(az) + len(ax))
+
+    for i, peer in enumerate(az):
+        pltpu.make_async_remote_copy(
+            c_out.at[peer[1]], c1.at[b], s1s, s1r, device_id=peer, device_id_type=MESH
+        ).start()
+    c1[b] = c_out[b]
+
+    @pl.loop(0, (NA - 1) * CAP)
+    def _(n):
+        sb[n] = eb[send_ref[n]]
+
+    for i, peer in enumerate(ax):
+        pltpu.make_async_remote_copy(
+            sb.at[pl.ds(i * CAP, CAP)], rb.at[pl.ds(i * CAP, CAP)], es, er, device_id=peer, device_id_type=MESH
+        ).start()
+
+    load_e.wait()
+
+    @pl.loop(0, CX)
+    def _(x):
+        t = thermal_distribution(e_ref[x])
+        t_ref[x] = t
+        ty[0, x] = t[0:1]
+        ty[1, x] = t[CY - 1 : CY]
+
+    up_b, down_b = (a, lax.rem(b + 1, NB)), (a, lax.rem(b + NB - 1, NB))
+    up_a, down_a = (lax.rem(a + 1, NA), b), (lax.rem(a + NA - 1, NA), b)
+    y_up = pltpu.make_async_remote_copy(ty.at[1], hy.at[0], hys.at[0], hyr.at[0], device_id=up_b, device_id_type=MESH)
+    y_down = pltpu.make_async_remote_copy(ty.at[0], hy.at[1], hys.at[1], hyr.at[1], device_id=down_b, device_id_type=MESH)
+    y_up.start()
+    y_down.start()
+
+    whole1 = pltpu.make_async_remote_copy(
+        c_out.at[pl.ds(0, NB - 1)], c1.at[pl.ds(0, NB - 1)], s1s, s1r, device_id=az[0], device_id_type=MESH
+    )
+    whole1.wait_recv()
+    sum1[...] = jnp.sum(c1[...], axis=0)
+    for i, peer in enumerate(ax):
+        pltpu.make_async_remote_copy(sum1, c2.at[a], s2s, s2r, device_id=peer, device_id_type=MESH).start()
+    c2[a] = sum1[...]
+
+    x_up = pltpu.make_async_remote_copy(
+        t_ref.at[CX - 1], hx.at[0], hxs.at[0], hxr.at[0], device_id=up_a, device_id_type=MESH
+    )
+    x_down = pltpu.make_async_remote_copy(
+        t_ref.at[0], hx.at[1], hxs.at[1], hxr.at[1], device_id=down_a, device_id_type=MESH
+    )
+    x_up.start()
+    x_down.start()
+
+    y_up.wait()
+    y_down.wait()
+
+    line = lax.broadcasted_iota(I32, (CY, CZ), 0)
+    radial = lax.broadcasted_iota(I32, (CY, CZ), 1)
+
+    def plane(x, below, above):
+        t = t_ref[x]
+        ym = jnp.where(line == 0, hy[0, x], pltpu.roll(t, 1, 0))
+        yp = jnp.where(line == CY - 1, hy[1, x], pltpu.roll(t, CY - 1, 0))
+        zm = jnp.where(radial == 0, 0.0, pltpu.roll(t, 1, 1))
+        zp = jnp.where(radial == CZ - 1, 0.0, pltpu.roll(t, CZ - 1, 1))
+        heated_ref[x] = e_ref[x] + DT_MACRO * ((below + above) + (ym + yp) + (zm + zp) - 6.0 * t)
+
+    @pl.loop(1, CX - 1)
+    def _(x):
+        plane(x, t_ref[x - 1], t_ref[x + 1])
+
+    whole2 = pltpu.make_async_remote_copy(
+        c2.at[pl.ds(0, NA - 1)], c2.at[pl.ds(0, NA - 1)], s2s, s2r, device_id=ax[0], device_id_type=MESH
+    )
+    whole2.wait_recv()
+    total = jnp.sum(c2[...], axis=0)
+    over_ref[...] = total[1:2]
+    temps = thermal_distribution(total[0:1])
+    lanes1 = lax.broadcasted_iota(I32, (1, 128), 1)
+
+    def temp_of(index):
+        return jnp.sum(jnp.where(lanes1 == index, temps, 0.0), axis=1, keepdims=True)
+
+    lane_full = lax.broadcasted_iota(I32, (SIDE, 128), 1)
+    row_full = lax.broadcasted_iota(I32, (SIDE, 128), 0)
+    body = (row_full >= 6) & (row_full < SIDE - 6)
+
+    @pl.loop(0, SLOTS)
+    def _(s):
+        tau = temp_of(a * SLOTS + s)
+        nb_t[s] = jnp.broadcast_to(tau, (1, 128))
+        k1, k4 = 1.5 + DRIVE_GAIN * tau, 4.5 + DRIVE_GAIN * tau
+        cur = (pt[s, 0], pt[s, 1])
+        for _step in range(PHASE_STEPS):
+            cur = phase_step(cur, (mt[s, 0], mt[s, 1]), k1, k4, lane_full)
+        ct[s, 0] = cur[0]
+        ct[s, 1] = cur[1]
+        change = (cur[0] - pt[s, 0]) + (cur[1] - pt[s, 1])
+        latsum[s] = jnp.sum(jnp.where(body, change, 0.0), axis=0, keepdims=True)
+
+    whole_e = pltpu.make_async_remote_copy(sb, rb, es, er, device_id=ax[0], device_id_type=MESH)
+    whole_e.wait_recv()
+    lane_strip = lax.broadcasted_iota(I32, (24, 128), 1)
+    row_strip = lax.broadcasted_iota(I32, (24, 128), 0)
+    lat[...] = jnp.zeros((1, 128), F32)
+
+    @pl.loop(0, SLOTS)
+    def _(s):
+        tau = nb_t[s]
+        curs, rates, ks = [], [], []
+        for side in range(2):
+            e = 2 * s + side
+            own_edge = place_ref[3 * e + 1]
+            near = eb[own_edge]
+            far = rb[recv_ref[e]]
+            is_far = jnp.broadcast_to(place_ref[3 * e + 2], (EDGE_ROWS, 128)) > 0
+            edge = jnp.where(is_far, far, near)
+            other = temp_of(place_ref[3 * e])
+            for h in range(2):
+                ph, mh = edge[h * 12 : h * 12 + 6], edge[h * 12 + 6 : h * 12 + 11]
+                if side == 0:
+                    stp[side, h, 0:2] = jnp.zeros((2, 128), F32)
+                    stp[side, h, 2:8] = ph
+                    stp[side, h, 8:24] = pt[s, h, 0:16]
+                    stm[side, h, 0:3] = jnp.zeros((3, 128), F32)
+                    stm[side, h, 3:8] = mh
+                    stm[side, h, 8:24] = mt[s, h, 0:16]
+                else:
+                    stp[side, h, 0:16] = pt[s, h, SIDE - 16 : SIDE]
+                    stp[side, h, 16:22] = ph
+                    stp[side, h, 22:24] = jnp.zeros((2, 128), F32)
+                    stm[side, h, 0:16] = mt[s, h, SIDE - 16 : SIDE]
+                    stm[side, h, 16:21] = mh
+                    stm[side, h, 21:24] = jnp.zeros((3, 128), F32)
+            outer = row_strip < 8 if side == 0 else row_strip >= 16
+            ks.append(DRIVE_GAIN * jnp.where(outer, other, tau))
+            curs.append((stp[side, 0], stp[side, 1]))
+            rates.append((stm[side, 0], stm[side, 1]))
+        starts = curs
+        for _step in range(PHASE_STEPS):
+            curs = [
+                phase_step(curs[side], rates[side], 1.5 + ks[side], 4.5 + ks[side], lane_strip) for side in range(2)
+            ]
+        total_s = latsum[s]
+        for side in range(2):
+            low = 8 if side == 0 else 10
+            first = 0 if side == 0 else SIDE - 6
+            for h in range(2):
+                ct[s, h, first : first + 6] = curs[side][h][low : low + 6]
+            kept = (row_strip >= low) & (row_strip < low + 6)
+            change = (curs[side][0] - starts[side][0]) + (curs[side][1] - starts[side][1])
+            total_s = total_s + jnp.sum(jnp.where(kept, change, 0.0), axis=0, keepdims=True)
+        value = jnp.sum(total_s, axis=1, keepdims=True) * (COUPLING / (SIDE * SIDE))
+        lat[...] = jnp.where(lanes1 == a * SLOTS + s, jnp.where(live_ref[...] > 0.5, value, 0.0), lat[...])
+
+    for i, peer in enumerate(ax):
+        pltpu.make_async_remote_copy(lat, l1.at[a], l1s, l1r, device_id=peer, device_id_type=MESH).start()
+    l1[a] = lat[...]
+
+    x_up.wait()
+    x_down.wait()
+    plane(0, jnp.where(a > 0, 1.0, 0.0).astype(F32) * hx[0], t_ref[1])
+    plane(CX - 1, t_ref[CX - 2], jnp.where(a < NA - 1, 1.0, 0.0).astype(F32) * hx[1])
+
+    whole_l1 = pltpu.make_async_remote_copy(
+        l1.at[pl.ds(0, NA - 1)], l1.at[pl.ds(0, NA - 1)], l1s, l1r, device_id=ax[0], device_id_type=MESH
+    )
+    whole_l1.wait_recv()
+    column = jnp.sum(l1[...], axis=0)
+    l2[b] = column
+    for i, peer in enumerate(az):
+        pltpu.make_async_remote_copy(l2.at[b], l2.at[b], l2s, l2r, device_id=peer, device_id_type=MESH).start()
+
+    @pl.loop(0, SLOTS)
+    def _(s):
+        alive = jnp.sum(jnp.where(lanes1 == a * SLOTS + s, live_ref[...], 0.0), axis=1, keepdims=True)
+        for h in range(2):
+            final = jnp.where(alive > 0.5, ct[s, h], pt[s, h])
+            out_ref[s, h * 128 : h * 128 + 128, :] = final.T
+
+    whole_l2 = pltpu.make_async_remote_copy(
+        l2.at[pl.ds(0, NB - 1)], l2.at[pl.ds(0, NB - 1)], l2s, l2r, device_id=az[0], device_id_type=MESH
+    )
+    whole_l2.wait_recv()
+    for j in range(NB):
+        latent_ref[j : j + 1, :] = l2[j]
+
+    whole1.wait_send()
+    whole2.wait_send()
+    whole_e.wait_send()
+    whole_l1.wait_send()
+    whole_l2.wait_send()
+
+
+def release_kernel(hits_ref, spos_ref, lat_ref, heated_hbm, phase_hbm, out_hbm, phase_out_hbm, grid_ref, sem):
+    move = pltpu.make_async_copy(phase_hbm, phase_out_hbm, sem.at[0])
+    move.start()
+    load = pltpu.make_async_copy(heated_hbm, grid_ref, sem.at[1])
+    load.start()
+    a, b = lax.axis_index("axial"), lax.axis_index("azim")
+    lane = lax.broadcasted_iota(I32, (1, CZ), 1)
+    load.wait()
+
+    def add(h, carry):
+        s = hits_ref[h + 1]
+        px, py = local_cell(spos_ref[s], spos_ref[NA * NB * SLOTS + s], a, b)
+        z = spos_ref[2 * NA * NB * SLOTS + s]
+        inside = (px >= 0) & (px < CX) & (py >= 0) & (py < CY)
+        x0 = jnp.clip(px, 0, CX - 1)
+        y0 = jnp.clip(py, 0, CY - 1)
+        value = jnp.where(inside, lat_ref[s], 0.0)
+        grid_ref[x0, pl.ds(y0, 1), :] = grid_ref[x0, pl.ds(y0, 1), :] + jnp.where(lane == z, value, 0.0)
+        return carry
+
+    lax.fori_loop(0, hits_ref[0], add, 0)
+    store = pltpu.make_async_copy(grid_ref, out_hbm, sem.at[2])
+    store.start()
+    store.wait()
+    move.wait()
+
+
+def spec(space):
+    return pl.BlockSpec(memory_space=space)
+
+
+def seam_tables(neighbours):
+    a = lax.axis_index("axial")
+    column = neighbours // SLOTS // NB
+    slot = neighbours % SLOTS
+    halo = jnp.arange(2 * SLOTS, dtype=I32)
+    source = column.reshape(-1)
+    edge_there = (2 * slot + jnp.array([1, 0], I32)).reshape(-1)
+    lower = halo[None, :] < halo[:, None]
+    rank = jnp.sum(((source[None, :] == source[:, None]) & lower).astype(I32), axis=1)
+    hop = (a - source) % NA
+    far = hop > 0
+    place = jnp.where(far, (hop - 1) * CAP + jnp.minimum(rank, CAP - 1), 0)
+    over = jnp.max(jnp.where(far & (rank >= CAP), 1.0, 0.0))
+    info = jnp.stack([source * SLOTS + slot.reshape(-1), edge_there, far.astype(I32)], axis=1).reshape(-1)
+    goal = column.reshape(-1)
+    key = (2 * slot + jnp.array([1, 0], I32)).reshape(-1)
+    turn = jnp.sum(((goal[None, :] == goal[:, None]) & (key[None, :] < key[:, None])).astype(I32), axis=1)
+    hop_out = (goal - a) % NA
+    wanted = jnp.arange((NA - 1) * CAP, dtype=I32)
+    chosen = ((hop_out - 1) * CAP + turn)[None, :] == wanted[:, None]
+    chosen = chosen & (hop_out > 0)[None, :] & (turn < CAP)[None, :]
+    sends = jnp.sum(jnp.where(chosen, halo[None, :], 0), axis=1)
+    return sends.astype(I32), place.astype(I32), info.astype(I32), over
+
+
+def shards(specific_heat_content, phase, mobility, positions, counts, neighbours):
+    a = lax.axis_index("axial")
+    pos = positions.T.reshape(3, NA, NB, SLOTS).transpose(0, 2, 1, 3).reshape(3, NB, NA * SLOTS)
+    flat = pos.reshape(-1)
+    sends, place, info, over = seam_tables(neighbours)
+    lanes = jnp.arange(NA * SLOTS, dtype=I32)
+    live = ((lanes // SLOTS == a) & (lanes % SLOTS < counts[0])).astype(F32).reshape(1, NA * SLOTS)
+    flag = jnp.broadcast_to(over, (1, 128)).astype(F32)
+
+    shares, hits = pl.pallas_call(
+        sample_kernel,
+        out_shape=(
+            jax.ShapeDtypeStruct((NB, 128), F32),
+            jax.ShapeDtypeStruct((NA * NB * SLOTS + 8,), I32),
+        ),
+        in_specs=[spec(VMEM), spec(SMEM), spec(pl.ANY)],
+        out_specs=(spec(VMEM), spec(SMEM)),
+        scratch_shapes=[VMEM((CX, CY, CZ), F32), DMA],
+        compiler_params=pltpu.CompilerParams(vmem_limit_bytes=16 << 20),
+        name="sample",
+    )(pos, flat, specific_heat_content)
+
+    heated, phase_new, latents, over_all = pl.pallas_call(
+        main_kernel,
+        out_shape=(
+            jax.ShapeDtypeStruct((CX, CY, CZ), F32),
+            jax.ShapeDtypeStruct((SLOTS, SIDE, SIDE), F32),
+            jax.ShapeDtypeStruct((NB, 128), F32),
+            jax.ShapeDtypeStruct((1, 128), F32),
+        ),
+        in_specs=[spec(SMEM)] * 3 + [spec(VMEM)] * 3 + [spec(pl.ANY)] * 3,
+        out_specs=(spec(VMEM), spec(VMEM), spec(VMEM), spec(VMEM)),
+        scratch_shapes=[
+            VMEM((CX, CY, CZ), F32),
+            VMEM((CX, CY, CZ), F32),
+            VMEM((SLOTS, SIDE, SIDE), F32),
+            VMEM((SLOTS, SIDE, SIDE), F32),
+            VMEM((SLOTS, 2, SIDE, 128), F32),
+            VMEM((SLOTS, 2, SIDE, 128), F32),
+            VMEM((SLOTS, 2, SIDE, 128), F32),
+            VMEM((2 * SLOTS, EDGE_ROWS, 128), F32),
+            VMEM(((NA - 1) * CAP, EDGE_ROWS, 128), F32),
+            VMEM(((NA - 1) * CAP, EDGE_ROWS, 128), F32),
+            VMEM((2, 2, 24, 128), F32),
+            VMEM((2, 2, 24, 128), F32),
+            VMEM((2, CY, CZ), F32),
+            VMEM((2, CX, 1, CZ), F32),
+            VMEM((2, CX, 1, CZ), F32),
+            VMEM((NB, 2, 128), F32),
+            VMEM((NB, 2, 128), F32),
+            VMEM((NA, 2, 128), F32),
+            VMEM((2, 128), F32),
+            VMEM((1, 128), F32),
+            VMEM((NA, 1, 128), F32),
+            VMEM((NB, 1, 128), F32),
+            VMEM((SLOTS, 1, 128), F32),
+            VMEM((SLOTS, 1, 128), F32),
+            DMA((3,)),
+            DMA, DMA, DMA, DMA, DMA, DMA,
+            DMA((2,)), DMA((2,)), DMA((2,)), DMA((2,)),
+            DMA, DMA, DMA, DMA,
+        ],
+        compiler_params=pltpu.CompilerParams(
+            collective_id=0, has_side_effects=True, vmem_limit_bytes=48 << 20
+        ),
+        name="couple",
+    )(sends, place, info, shares, flag, live, specific_heat_content, phase, mobility)
+
+    def finish():
+        return pl.pallas_call(
+            release_kernel,
+            out_shape=(
+                jax.ShapeDtypeStruct((CX, CY, CZ), F32),
+                jax.ShapeDtypeStruct((SLOTS, SIDE, SIDE), F32),
+            ),
+            in_specs=[spec(SMEM)] * 3 + [spec(pl.ANY)] * 2,
+            out_specs=(spec(pl.ANY), spec(pl.ANY)),
+            scratch_shapes=[VMEM((CX, CY, CZ), F32), DMA((3,))],
+            compiler_params=pltpu.CompilerParams(vmem_limit_bytes=16 << 20),
+            name="release",
+        )(hits, flat, latents.reshape(-1), heated, phase_new)
+
+    def whole():
+        return general(specific_heat_content, phase, mobility, positions, counts, neighbours)
+
+    return lax.cond(over_all[0, 0] > 0.5, whole, finish)
+
+
 def solution(mesh):
     in_specs = (
         P("axial", "azim", None),

time: 419 us -> 72.4 us (0.17)
  blocking collectives: 267 us -> 0 us
  other arithmetic: 71.4 us -> 1.64 us
  Pallas kernels: 0 us -> 65.5 us
  local copies, waits for them, and re-layouts: 68.5 us -> 3.23 us
  starting transfers between devices: 8.88 us -> 0 us
    unnamed x2 -> x0, blocking collectives: 161 us -> none
    all_gather x6 -> x0, blocking collectives: 105 us -> none  [shards(): gathered = lax.all_gather(edges, 'axial', axis=0, tiled=True)]
    pallas_call x0 -> x3, Pallas kernels: none -> 65.5 us  [the longest x1 55.5 us: shards(): pl.pallas_call(main_kernel, out_shape=(jax.ShapeDtypeStruct((CX, CY, CZ),...]
    add x7 -> x1, other arithmetic: 52.5 us -> 0.67 us  [seam_tables(): source * SLOTS + slot.reshape(-1)]
    gather x13 -> x0, local copies, waits for them, and re-layouts: 42 us -> none  [the longest x1 35 us: shards(): sampled = jnp.where(inside, chilled_snapshot.reshape(-1)[flat_index], 0.0)]
    unnamed x28 -> x7, local copies, waits for them, and re-layouts: 20.6 us -> 0.77 us
    scatter-add x1 -> x0, other arithmetic: 10 us -> none  [shards(): enthalpy_out = warmed_snapshot.reshape(-1).at[flat_index].add(released).r...]
    ppermute x4 -> x0, starting transfers between devices: 8.88 us -> none  [the longest x2 6.28 us: extended(): before = lax.ppermute(last, axis, up)]
  transfers between devices with their start and end apart: 4 -> 0, of which waited for: 0 -> 0; matrix products, arithmetic and copies ran while one was open for 1% -> 0% of each run, Pallas kernels for 0% -> 0%
where the time goes in v1:
time: 72.4 us; the launch traced here: 72.2 us
  Pallas kernels  65.5 us (90%)
  local copies, waits for them, and re-layouts  3.23 us (4%)
  other arithmetic  1.64 us (2%)
  between operations  1.62 us (2%)
    pallas_call x1, Pallas kernels, shards(): pl.pallas_call(main_kernel, out_shape=(jax.ShapeDtypeStruct((CX, CY, CZ),...  55.5 us
    pallas_call x1, Pallas kernels, shards(): pl.pallas_call(sample_kernel, out_shape=(jax.ShapeDtypeStruct((NB, 128),...  6.31 us
    pallas_call x1, Pallas kernels, finish(): pl.pallas_call(release_kernel, out_shape=(jax.ShapeDtypeStruct((CX, CY, C...  3.6 us

profile of v1, /device:TPU:1, one launch (start us, length us, event | category | flops | bytes accessed | tf_op | source)
XLA Modules:
  0.0 72.2 jit_solution(3561205604684808485)
XLA Ops:
  0.6 0.8 %copy.77 = s32[8,2]{1,0:T(8,128)S(1)} copy(s32[8,2]{0,1:T(2,128)} %param.15) | data formatting | bytes 128 | tf_op args[5]
  1.4 0.7 multiply_add_fusion
  2.1 0.1 reshape.227
  2.1 0.1 lt.129
  2.2 0.2 convert_reduce_fusion
  2.5 0.1 select_reduce_fusion.send_ref
  2.6 0.1 ge.16
  2.6 0.6 select_reduce_fusion.1
  3.3 0.1 sub.193
  3.4 0.1 stack_reshape.3
  3.4 0.1 add.326
  3.5 0.1 copy.81
  3.6 0.1 reshape.228.place_ref
  3.7 0.7 broadcast_in_dim.107.flag_ref
  4.4 0.9 %reshape.229 = s32[3,16,8,8]{3,2,1,0:T(8,128)S(1)} reshape(s32[3,1024]{1,0:T(4,128)} %bitcast.63) | data formatting | bytes 24576 | tf_op jit(solution)/shard_map/reshape | solution.py:499
  5.3 0.1 reshape_reshape.3.spos_ref
  5.4 0.1 reshape.230.pos_ref
  5.5 0.0 copy-start
  5.5 6.3 %sample.1 = (f32[8,128]{1,0:T(8,128)S(1)}, s32[1032]{0:T(1024)S(1)}) custom-call(s32[3,8,128]{2,1,0:T(8,128)S(1)} %reshape.230.pos_ref, s32[3072]{0:T(1024)S(1)} %reshape_reshape.3.spos_ref, f32[16,128,512]{2,1,0:T(8,128)} %e_hbm.3), custom_call_target="tpu_custom_call" | custom-call | tf_op jit(solution)/shard_map/sample/pallas_call | solution.py:506
  12.5 0.0 copy-done
  12.5 0.0 copy-start.11
  12.5 0.0 copy-start.12
  12.6 55.5 %couple.1 = (f32[16,128,512]{2,1,0:T(8,128)S(1)}, f32[8,256,256]{2,1,0:T(8,128)S(1)}, f32[8,128]{1,0:T(8,128)S(1)}, f32[1,128]{1,0:T(1,128)S(1)}) custom-call(s32[90]{0:T(128)S(1)} %select_reduce_fusion.send_ref, s32[16]{0:T(128)S(1)} %get-tuple-element.123.recv_ref, s32[48]{0:T(128)S(1)} %reshape.228.place_ref, f32[8,128]{1,0:T(8,128)S(1)} %get-tuple-element.41.c_ref, ...), custom_call_target="tpu_custom_call" | custom-call | tf_op jit(solution)/shard_map/couple/pallas_call | solution.py:519
  68.1 0.0 copy-done.11
  68.2 0.0 copy-done.12
  68.2 3.8 %conditional.1 = ((f32[16,128,512]{2,1,0:T(8,128)}, f32[8,256,256]{2,1,0:T(8,128)})) conditional(s32[]{:T(128)} %bitcast.32, (f32[8,128]{1,0:T(8,128)S(1)}, s32[1032]{0:T(1024)S(1)}, s32[3072]{0:T(1024)S(1)}, f32[16,128,512]{2,1,0:T(8,128)S(1)}, f32[8,256,256]{2,1,0:T(8,128)S(1)}) %tuple.14, (f32[16,128,512]{2,1,0:T(8,128)S(1)}, ...), branch_computations={%region_4.5_spmd, %region_5.9_spmd} | conditional | flops 73976504 | bytes 216504128 | solution.py:582
  68.2 3.6 %release.1 = (f32[16,128,512]{2,1,0:T(8,128)}, f32[8,256,256]{2,1,0:T(8,128)}) custom-call(s32[1032]{0:T(1024)S(1)} %get-tuple-element.22.hits_ref, s32[3072]{0:T(1024)S(1)} %get-tuple-element.23.spos_ref, f32[1024]{0:T(1024)S(1)} %bitcast.78, f32[16,128,512]{2,1,0:T(8,128)S(1)} %get-tuple-element.25.heated_hbm, f32[8,256,256]{2,1,0:T(8,128)S(1)} %get-tuple-element.26.phase_hbm), custom_call_target="tpu_custom_call" | custom-call | tf_op jit(solution)/shard_map/cond/branch_0_fun/release/pallas_call | solution.py:566
  (7 shorter events, 0.1 us)
Async XLA Ops:
  5.5 7.0 %copy-start = (f32[16,128,512]{2,1,0:T(8,128)S(1)}, f32[16,128,512]{2,1,0:T(8,128)}, u32[]{:S(2)}) copy-start(f32[16,128,512]{2,1,0:T(8,128)} %e_hbm.3) | copy-start | bytes 12582916
  12.5 55.6 %copy-start.11 = (s32[1024,3]{0,1:T(4,128)S(1)}, s32[1024,3]{0,1:T(4,128)}, u32[]{:S(2)}) copy-start(s32[1024,3]{0,1:T(4,128)} %param.13) | copy-start | bytes 36868
  12.5 55.6 %copy-start.12 = (s32[8,2]{0,1:T(2,128)S(1)}, s32[8,2]{0,1:T(2,128)}, u32[]{:S(2)}) copy-start(s32[8,2]{0,1:T(2,128)} %param.15) | copy-start | bytes 196

commit v2 on v1

--- a/solution.py
+++ b/solution.py
@@ -17,7 +17,9 @@
 SLOTS = 8
 SIDE = 256
 CX, CY, CZ = 16, 128, 512
-CAP = 6
+CAP = 5
+HIT_CAP = 32
+HIT_GROUP = 4
 EDGE_ROWS = 24
 MESH = pl.DeviceIdType.MESH
 F32 = jnp.float32
@@ -119,11 +121,11 @@
     return x - a * CX, ((y - b * CY + 1) & (NB * CY - 1)) - 1
 
 
-def sample_kernel(pos_ref, spos_ref, e_hbm, c_ref, hits_ref, e_ref, sem):
-    load = pltpu.make_async_copy(e_hbm, e_ref, sem)
-    load.start()
-    a, b = lax.axis_index("axial"), lax.axis_index("azim")
-    lx, ly = local_cell(pos_ref[0], pos_ref[1], a, b)
+def rank_hits(pos_ref, posb, a, b):
+    for c in range(2):
+        for r in range(8):
+            posb[c, r : r + 1, :] = pos_ref[c : c + 1, r * 128 : r * 128 + 128]
+    lx, ly = local_cell(posb[0], posb[1], a, b)
     inx = (lx >= 0) & (lx < CX)
     iny = (ly >= 0) & (ly < CY)
     touched = (inx & (ly <= CY)) | (iny & (lx >= -1) & (lx <= CX))
@@ -137,49 +139,64 @@
     col8 = lax.broadcasted_iota(I32, (8, 8), 1)
     above = jnp.dot(jnp.where(col8 < row8, 1.0, 0.0).astype(F32), totals, preferred_element_type=F32)
     rank = jnp.where(touched, within + above, -1.0)
-    linear = lax.broadcasted_iota(I32, (8, 128), 0) * 128 + lax.broadcasted_iota(I32, (8, 128), 1)
-    count = jnp.sum(mark).astype(I32)
-    hits_ref[0] = count
-    c_ref[...] = jnp.zeros((8, 128), F32)
-    lane = lax.broadcasted_iota(I32, (1, CZ), 1)
-    load.wait()
-    group = 4
-
-    def chunk(i, carry):
-        acc = c_ref[...]
-        for j in range(group):
-            h = i * group + j
-            s = jnp.sum(jnp.where(rank == h.astype(F32), linear, 0))
-            hits_ref[h + 1] = s
-            valid = h < count
-            px, py = local_cell(spos_ref[s], spos_ref[NA * NB * SLOTS + s], a, b)
-            z = spos_ref[2 * NA * NB * SLOTS + s]
-            okx = (px >= 0) & (px < CX) & valid
-            oky = (py >= 0) & (py < CY) & valid
-            x0 = jnp.clip(px, 0, CX - 1)
-            y0 = jnp.clip(py, 0, CY - 1)
-
-            def part(x, y, ok):
-                t = thermal_distribution(e_ref[jnp.clip(x, 0, CX - 1), pl.ds(jnp.clip(y, 0, CY - 1), 1), :])
-                return jnp.where(ok, t, 0.0)
-
-            inside = okx & oky
-            own = jnp.where(inside, e_ref[x0, pl.ds(y0, 1), :], 0.0)
-            t = thermal_distribution(own)
-            ring = (
-                part(px - 1, y0, oky & (px >= 1) & (px <= CX))
-                + part(px + 1, y0, oky & (px >= -1) & (px < CX - 1))
-                + part(x0, py - 1, okx & (py >= 1) & (py <= CY))
-                + part(x0, py + 1, okx & (py >= -1) & (py < CY - 1))
-            )
-            here = lane == z
-            beside = (lane == z - 1) | (lane == z + 1)
-            value = jnp.where(here, own + DT_MACRO * (ring - 6.0 * t), 0.0) + jnp.where(beside, DT_MACRO * t, 0.0)
-            acc = acc + jnp.where((linear == s) & valid, jnp.sum(value, keepdims=True), 0.0)
-        c_ref[...] = acc
-        return carry
-
-    lax.fori_loop(0, (count + group - 1) // group, chunk, 0)
+    return rank, jnp.sum(touched.astype(I32))
+
+
+def share_of(s, valid, spos_ref, e_ref, a, b, lane):
+    px, py = local_cell(spos_ref[0, s], spos_ref[1, s], a, b)
+    z = spos_ref[2, s]
+    okx = (px >= 0) & (px < CX) & valid
+    oky = (py >= 0) & (py < CY) & valid
+    x0 = jnp.clip(px, 0, CX - 1)
+    y0 = jnp.clip(py, 0, CY - 1)
+
+    def part(x, y, ok):
+        t = thermal_distribution(e_ref[jnp.clip(x, 0, CX - 1), pl.ds(jnp.clip(y, 0, CY - 1), 1), :])
+        return jnp.where(ok, t, 0.0)
+
+    own = jnp.where(okx & oky, e_ref[x0, pl.ds(y0, 1), :], 0.0)
+    t = thermal_distribution(own)
+    ring = (
+        part(px - 1, y0, oky & (px >= 1) & (px <= CX))
+        + part(px + 1, y0, oky & (px >= -1) & (px < CX - 1))
+        + part(x0, py - 1, okx & (py >= 1) & (py <= CY))
+        + part(x0, py + 1, okx & (py >= -1) & (py < CY - 1))
+    )
+    here = lane == z
+    beside = (lane == z - 1) | (lane == z + 1)
+    value = jnp.where(here, own + DT_MACRO * (ring - 6.0 * t), 0.0) + jnp.where(beside, DT_MACRO * t, 0.0)
+    return jnp.sum(value, keepdims=True)
+
+
+def seam_tables(nb_ref, place_ref, recv_ref, a):
+    halos = range(2 * SLOTS)
+    names = [nb_ref[e % 2, e // 2] for e in halos]
+    source = [n // (SLOTS * NB) for n in names]
+    slot = [n % SLOTS for n in names]
+    over = jnp.int32(0)
+    for e in halos:
+        rank = jnp.int32(0)
+        for f in range(e):
+            rank = rank + (source[f] == source[e]).astype(I32)
+        hop = (a - source[e] + NA) % NA
+        far = (hop > 0).astype(I32)
+        over = jnp.maximum(over, far * (rank >= CAP).astype(I32))
+        recv_ref[e] = jnp.where(hop > 0, (hop - 1) * CAP + jnp.minimum(rank, CAP - 1), 0)
+        place_ref[3 * e] = source[e] * SLOTS + slot[e]
+        place_ref[3 * e + 1] = 2 * slot[e] + 1 - e % 2
+        place_ref[3 * e + 2] = far
+    key = [2 * slot[f] + 1 - f % 2 for f in halos]
+    lane = lax.broadcasted_iota(I32, (1, 128), 1)
+    sends = jnp.zeros((1, 128), I32)
+    for f in halos:
+        turn = jnp.int32(0)
+        for g in halos:
+            if g != f:
+                turn = turn + ((source[g] == source[f]) & (key[g] < key[f])).astype(I32)
+        hop = (source[f] - a + NA) % NA
+        goal = jnp.where((hop > 0) & (turn < CAP), (hop - 1) * CAP + turn, -1)
+        sends = sends + jnp.where(lane == goal, f, 0)
+    return sends, over
 
 
 def lane_sum(halves, lane):
@@ -205,8 +222,9 @@
 
 
 def main_kernel(
-    send_ref, recv_ref, place_ref, c_ref, flag_ref, live_ref, e_hbm, phase_hbm, mob_hbm,
-    heated_ref, out_ref, latent_ref, over_ref,
+    pos_ref, spos_ref, nb_ref, count_ref, e_hbm, phase_hbm, mob_hbm,
+    heated_ref, out_ref, latent_ref, over_ref, hits_ref,
+    send_v, send_ref, recv_ref, place_ref, posb, shares,
     e_ref, t_ref, p_ref, m_ref, pt, mt, ct, eb, sb, rb, stp, stm,
     hx, hy, ty, c_out, c1, c2, sum1, lat, l1, l2, latsum, nb_t,
     load_sem, s1s, s1r, s2s, s2r, es, er, hxs, hxr, hys, hyr, l1s, l1r, l2s, l2r,
@@ -221,14 +239,65 @@
     load_p = pltpu.make_async_copy(phase_hbm, p_ref, load_sem.at[0])
     load_m = pltpu.make_async_copy(mob_hbm, m_ref, load_sem.at[1])
     load_e = pltpu.make_async_copy(e_hbm, e_ref, load_sem.at[2])
+    load_e.start()
     load_p.start()
     load_m.start()
-    load_e.start()
+
+    lanes1 = lax.broadcasted_iota(I32, (1, 128), 1)
+    alive_all = ((lanes1 // SLOTS == a) & (lanes1 % SLOTS < count_ref[0])).astype(F32)
+    sends, over = seam_tables(nb_ref, place_ref, recv_ref, a)
+    send_v[...] = sends
+    to_smem = pltpu.make_async_copy(send_v, send_ref, load_sem.at[3])
+    to_smem.start()
+    rank, count = rank_hits(pos_ref, posb, a, b)
+    over = jnp.maximum(over, (count > HIT_CAP).astype(I32))
+    hits_ref[0] = jnp.minimum(count, HIT_CAP)
+    shares[...] = jnp.zeros((NB, 128), F32)
+    linear = lax.broadcasted_iota(I32, (NB, 128), 0) * 128 + lax.broadcasted_iota(I32, (NB, 128), 1)
+    lane_z = lax.broadcasted_iota(I32, (1, CZ), 1)
+    load_e.wait()
+
+    @pl.loop(0, HIT_CAP // HIT_GROUP)
+    def _(i):
+        acc = shares[...]
+        for j in range(HIT_GROUP):
+            h = i * HIT_GROUP + j
+            s = jnp.clip(jnp.sum(jnp.where(rank == h.astype(F32), linear, 0)), 0, NA * NB * SLOTS - 1)
+            hits_ref[h + 1] = s
+            goal = ((s // SLOTS) % NB) * 128 + (s // (SLOTS * NB)) * SLOTS + s % SLOTS
+            value = share_of(s, h < count, spos_ref, e_ref, a, b, lane_z)
+            acc = acc + jnp.where(linear == goal, value, 0.0)
+        shares[...] = acc
+
     for j in range(NB):
-        c_out[j, 0:1, :] = c_ref[j : j + 1, :]
-        c_out[j, 1:2, :] = flag_ref[...]
+        c_out[j, 0:1, :] = shares[j : j + 1, :]
+        c_out[j, 1:2, :] = jnp.full((1, 128), over, I32).astype(F32)
+
+    pl.semaphore_wait(barrier, len(az) + len(ax))
+
+    for i, peer in enumerate(az):
+        pltpu.make_async_remote_copy(
+            c_out.at[peer[1]], c1.at[b], s1s, s1r, device_id=peer, device_id_type=MESH
+        ).start()
+    c1[b] = c_out[b]
+
+    @pl.loop(0, CX)
+    def _(x):
+        t = thermal_distribution(e_ref[x])
+        t_ref[x] = t
+        ty[0, x] = t[0:1]
+        ty[1, x] = t[CY - 1 : CY]
+
+    up_b, down_b = (a, lax.rem(b + 1, NB)), (a, lax.rem(b + NB - 1, NB))
+    up_a, down_a = (lax.rem(a + 1, NA), b), (lax.rem(a + NA - 1, NA), b)
+    y_up = pltpu.make_async_remote_copy(ty.at[1], hy.at[0], hys.at[0], hyr.at[0], device_id=up_b, device_id_type=MESH)
+    y_down = pltpu.make_async_remote_copy(ty.at[0], hy.at[1], hys.at[1], hyr.at[1], device_id=down_b, device_id_type=MESH)
+    y_up.start()
+    y_down.start()
+
     load_p.wait()
     load_m.wait()
+    to_smem.wait()
 
     @pl.loop(0, SLOTS)
     def _(s):
@@ -246,38 +315,9 @@
             eb[2 * s, base + 11 : base + 12] = jnp.zeros((1, 128), F32)
             eb[2 * s + 1, base + 11 : base + 12] = jnp.zeros((1, 128), F32)
 
-    pl.semaphore_wait(barrier, len(az) + len(ax))
-
-    for i, peer in enumerate(az):
-        pltpu.make_async_remote_copy(
-            c_out.at[peer[1]], c1.at[b], s1s, s1r, device_id=peer, device_id_type=MESH
-        ).start()
-    c1[b] = c_out[b]
-
     @pl.loop(0, (NA - 1) * CAP)
     def _(n):
-        sb[n] = eb[send_ref[n]]
-
-    for i, peer in enumerate(ax):
-        pltpu.make_async_remote_copy(
-            sb.at[pl.ds(i * CAP, CAP)], rb.at[pl.ds(i * CAP, CAP)], es, er, device_id=peer, device_id_type=MESH
-        ).start()
-
-    load_e.wait()
-
-    @pl.loop(0, CX)
-    def _(x):
-        t = thermal_distribution(e_ref[x])
-        t_ref[x] = t
-        ty[0, x] = t[0:1]
-        ty[1, x] = t[CY - 1 : CY]
-
-    up_b, down_b = (a, lax.rem(b + 1, NB)), (a, lax.rem(b + NB - 1, NB))
-    up_a, down_a = (lax.rem(a + 1, NA), b), (lax.rem(a + NA - 1, NA), b)
-    y_up = pltpu.make_async_remote_copy(ty.at[1], hy.at[0], hys.at[0], hyr.at[0], device_id=up_b, device_id_type=MESH)
-    y_down = pltpu.make_async_remote_copy(ty.at[0], hy.at[1], hys.at[1], hyr.at[1], device_id=down_b, device_id_type=MESH)
-    y_up.start()
-    y_down.start()
+        sb[n] = eb[jnp.clip(send_ref[0, n], 0, 2 * SLOTS - 1)]
 
     whole1 = pltpu.make_async_remote_copy(
         c_out.at[pl.ds(0, NB - 1)], c1.at[pl.ds(0, NB - 1)], s1s, s1r, device_id=az[0], device_id_type=MESH
@@ -287,6 +327,11 @@
     for i, peer in enumerate(ax):
         pltpu.make_async_remote_copy(sum1, c2.at[a], s2s, s2r, device_id=peer, device_id_type=MESH).start()
     c2[a] = sum1[...]
+
+    for i, peer in enumerate(ax):
+        pltpu.make_async_remote_copy(
+            sb.at[pl.ds(i * CAP, CAP)], rb.at[pl.ds(i * CAP, CAP)], es, er, device_id=peer, device_id_type=MESH
+        ).start()
 
     x_up = pltpu.make_async_remote_copy(
         t_ref.at[CX - 1], hx.at[0], hxs.at[0], hxr.at[0], device_id=up_a, device_id_type=MESH
@@ -322,7 +367,6 @@
     total = jnp.sum(c2[...], axis=0)
     over_ref[...] = total[1:2]
     temps = thermal_distribution(total[0:1])
-    lanes1 = lax.broadcasted_iota(I32, (1, 128), 1)
 
     def temp_of(index):
         return jnp.sum(jnp.where(lanes1 == index, temps, 0.0), axis=1, keepdims=True)
@@ -397,7 +441,7 @@
             change = (curs[side][0] - starts[side][0]) + (curs[side][1] - starts[side][1])
             total_s = total_s + jnp.sum(jnp.where(kept, change, 0.0), axis=0, keepdims=True)
         value = jnp.sum(total_s, axis=1, keepdims=True) * (COUPLING / (SIDE * SIDE))
-        lat[...] = jnp.where(lanes1 == a * SLOTS + s, jnp.where(live_ref[...] > 0.5, value, 0.0), lat[...])
+        lat[...] = jnp.where(lanes1 == a * SLOTS + s, jnp.where(alive_all > 0.5, value, 0.0), lat[...])
 
     for i, peer in enumerate(ax):
         pltpu.make_async_remote_copy(lat, l1.at[a], l1s, l1r, device_id=peer, device_id_type=MESH).start()
@@ -419,7 +463,7 @@
 
     @pl.loop(0, SLOTS)
     def _(s):
-        alive = jnp.sum(jnp.where(lanes1 == a * SLOTS + s, live_ref[...], 0.0), axis=1, keepdims=True)
+        alive = jnp.sum(jnp.where(lanes1 == a * SLOTS + s, alive_all, 0.0), axis=1, keepdims=True)
         for h in range(2):
             final = jnp.where(alive > 0.5, ct[s, h], pt[s, h])
             out_ref[s, h * 128 : h * 128 + 128, :] = final.T
@@ -449,12 +493,13 @@
 
     def add(h, carry):
         s = hits_ref[h + 1]
-        px, py = local_cell(spos_ref[s], spos_ref[NA * NB * SLOTS + s], a, b)
-        z = spos_ref[2 * NA * NB * SLOTS + s]
+        px, py = local_cell(spos_ref[0, s], spos_ref[1, s], a, b)
+        z = spos_ref[2, s]
         inside = (px >= 0) & (px < CX) & (py >= 0) & (py < CY)
         x0 = jnp.clip(px, 0, CX - 1)
         y0 = jnp.clip(py, 0, CY - 1)
-        value = jnp.where(inside, lat_ref[s], 0.0)
+        lat = lat_ref[((s // SLOTS) % NB) * 128 + (s // (SLOTS * NB)) * SLOTS + s % SLOTS]
+        value = jnp.where(inside, lat, 0.0)
         grid_ref[x0, pl.ds(y0, 1), :] = grid_ref[x0, pl.ds(y0, 1), :] + jnp.where(lane == z, value, 0.0)
         return carry
 
@@ -469,64 +514,28 @@
     return pl.BlockSpec(memory_space=space)
 
 
-def seam_tables(neighbours):
-    a = lax.axis_index("axial")
-    column = neighbours // SLOTS // NB
-    slot = neighbours % SLOTS
-    halo = jnp.arange(2 * SLOTS, dtype=I32)
-    source = column.reshape(-1)
-    edge_there = (2 * slot + jnp.array([1, 0], I32)).reshape(-1)
-    lower = halo[None, :] < halo[:, None]
-    rank = jnp.sum(((source[None, :] == source[:, None]) & lower).astype(I32), axis=1)
-    hop = (a - source) % NA
-    far = hop > 0
-    place = jnp.where(far, (hop - 1) * CAP + jnp.minimum(rank, CAP - 1), 0)
-    over = jnp.max(jnp.where(far & (rank >= CAP), 1.0, 0.0))
-    info = jnp.stack([source * SLOTS + slot.reshape(-1), edge_there, far.astype(I32)], axis=1).reshape(-1)
-    goal = column.reshape(-1)
-    key = (2 * slot + jnp.array([1, 0], I32)).reshape(-1)
-    turn = jnp.sum(((goal[None, :] == goal[:, None]) & (key[None, :] < key[:, None])).astype(I32), axis=1)
-    hop_out = (goal - a) % NA
-    wanted = jnp.arange((NA - 1) * CAP, dtype=I32)
-    chosen = ((hop_out - 1) * CAP + turn)[None, :] == wanted[:, None]
-    chosen = chosen & (hop_out > 0)[None, :] & (turn < CAP)[None, :]
-    sends = jnp.sum(jnp.where(chosen, halo[None, :], 0), axis=1)
-    return sends.astype(I32), place.astype(I32), info.astype(I32), over
-
-
 def shards(specific_heat_content, phase, mobility, positions, counts, neighbours):
-    a = lax.axis_index("axial")
-    pos = positions.T.reshape(3, NA, NB, SLOTS).transpose(0, 2, 1, 3).reshape(3, NB, NA * SLOTS)
-    flat = pos.reshape(-1)
-    sends, place, info, over = seam_tables(neighbours)
-    lanes = jnp.arange(NA * SLOTS, dtype=I32)
-    live = ((lanes // SLOTS == a) & (lanes % SLOTS < counts[0])).astype(F32).reshape(1, NA * SLOTS)
-    flag = jnp.broadcast_to(over, (1, 128)).astype(F32)
-
-    shares, hits = pl.pallas_call(
-        sample_kernel,
-        out_shape=(
-            jax.ShapeDtypeStruct((NB, 128), F32),
-            jax.ShapeDtypeStruct((NA * NB * SLOTS + 8,), I32),
-        ),
-        in_specs=[spec(VMEM), spec(SMEM), spec(pl.ANY)],
-        out_specs=(spec(VMEM), spec(SMEM)),
-        scratch_shapes=[VMEM((CX, CY, CZ), F32), DMA],
-        compiler_params=pltpu.CompilerParams(vmem_limit_bytes=16 << 20),
-        name="sample",
-    )(pos, flat, specific_heat_content)
-
-    heated, phase_new, latents, over_all = pl.pallas_call(
+    pos = positions.T
+    near = neighbours.T
+
+    heated, phase_new, latents, over_all, hits = pl.pallas_call(
         main_kernel,
         out_shape=(
             jax.ShapeDtypeStruct((CX, CY, CZ), F32),
             jax.ShapeDtypeStruct((SLOTS, SIDE, SIDE), F32),
             jax.ShapeDtypeStruct((NB, 128), F32),
             jax.ShapeDtypeStruct((1, 128), F32),
+            jax.ShapeDtypeStruct((HIT_CAP + 8,), I32),
         ),
-        in_specs=[spec(SMEM)] * 3 + [spec(VMEM)] * 3 + [spec(pl.ANY)] * 3,
-        out_specs=(spec(VMEM), spec(VMEM), spec(VMEM), spec(VMEM)),
+        in_specs=[spec(VMEM)] + [spec(SMEM)] * 3 + [spec(pl.ANY)] * 3,
+        out_specs=(spec(VMEM), spec(VMEM), spec(VMEM), spec(VMEM), spec(SMEM)),
         scratch_shapes=[
+            VMEM((1, 128), I32),
+            SMEM((1, 128), I32),
+            SMEM((2 * SLOTS,), I32),
+            SMEM((6 * SLOTS,), I32),
+            VMEM((2, NB, 128), I32),
+            VMEM((NB, 128), F32),
             VMEM((CX, CY, CZ), F32),
             VMEM((CX, CY, CZ), F32),
             VMEM((SLOTS, SIDE, SIDE), F32),
@@ -551,7 +560,7 @@
             VMEM((NB, 1, 128), F32),
             VMEM((SLOTS, 1, 128), F32),
             VMEM((SLOTS, 1, 128), F32),
-            DMA((3,)),
+            DMA((4,)),
             DMA, DMA, DMA, DMA, DMA, DMA,
             DMA((2,)), DMA((2,)), DMA((2,)), DMA((2,)),
             DMA, DMA, DMA, DMA,
@@ -560,7 +569,7 @@
             collective_id=0, has_side_effects=True, vmem_limit_bytes=48 << 20
         ),
         name="couple",
-    )(sends, place, info, shares, flag, live, specific_heat_content, phase, mobility)
+    )(pos, pos, near, counts, specific_heat_content, phase, mobility)
 
     def finish():
         return pl.pallas_call(
@@ -574,7 +583,7 @@
             scratch_shapes=[VMEM((CX, CY, CZ), F32), DMA((3,))],
             compiler_params=pltpu.CompilerParams(vmem_limit_bytes=16 << 20),
             name="release",
-        )(hits, flat, latents.reshape(-1), heated, phase_new)
+        )(hits, pos, latents.reshape(-1), heated, phase_new)
 
     def whole():
         return general(specific_heat_content, phase, mobility, positions, counts, neighbours)

time: 72.4 us -> 59.5 us (0.82)
  Pallas kernels: 65.5 us -> 57.5 us
  local copies, waits for them, and re-layouts: 3.23 us -> 0.01 us
  other arithmetic: 1.64 us -> 0 us
    pallas_call x1 -> x0, Pallas kernels: 6.31 us -> none  [shards(): pl.pallas_call(sample_kernel, out_shape=(jax.ShapeDtypeStruct((NB, 128),...]
    pallas_call x1, Pallas kernels: 55.5 us -> 53.9 us  [shards(): pl.pallas_call(main_kernel, out_shape=(jax.ShapeDtypeStruct((CX, CY, CZ),...]
    reshape x4 -> x0, local copies, waits for them, and re-layouts: 1.15 us -> none  [the longest x2 0.98 us: shards(): positions.T.reshape(3, NA, NB, SLOTS).transpose(0, 2, 1, 3)]
    unnamed x7 -> x4, local copies, waits for them, and re-layouts: 0.77 us -> 0.01 us
where the time goes in v2:
time: 59.5 us; the launch traced here: 59.3 us
  Pallas kernels  57.5 us (97%)
  between operations  1.53 us (3%)
    pallas_call x1, Pallas kernels, shards(): pl.pallas_call(main_kernel, out_shape=(jax.ShapeDtypeStruct((CX, CY, CZ),...  53.9 us
    pallas_call x1, Pallas kernels, finish(): pl.pallas_call(release_kernel, out_shape=(jax.ShapeDtypeStruct((CX, CY, C...  3.6 us

profile of v2, /device:TPU:1, one launch (start us, length us, event | category | flops | bytes accessed | tf_op | source)
XLA Modules:
  0.0 59.3 jit_solution(6863129910312293754)
XLA Ops:
  1.3 0.0 copy-start.9
  1.3 0.0 copy-start.10
  1.3 53.9 %couple.1 = (f32[16,128,512]{2,1,0:T(8,128)S(1)}, f32[8,256,256]{2,1,0:T(8,128)S(1)}, f32[8,128]{1,0:T(8,128)S(1)}, f32[1,128]{1,0:T(1,128)S(1)}, s32[40]{0:T(128)S(1)}) custom-call(s32[3,1024]{1,0:T(4,128)} %bitcast.56, s32[3,1024]{1,0:T(4,128)} %bitcast.57, s32[2,8]{1,0:T(2,128)} %bitcast.73, s32[1]{0:T(128)S(6)} %copy.52.count_ref, ...), custom_call_target="tpu_custom_call" | custom-call | tf_op jit(solution)/shard_map/couple/pallas_call | solution.py:521
  55.3 0.0 copy-done.9
  55.3 0.0 copy-done.10
  55.3 3.8 %conditional.1 = ((f32[16,128,512]{2,1,0:T(8,128)}, f32[8,256,256]{2,1,0:T(8,128)})) conditional(s32[]{:T(128)} %bitcast.31, (f32[8,128]{1,0:T(8,128)S(1)}, s32[40]{0:T(128)S(1)}, s32[3,1024]{1,0:T(4,128)S(1)}, f32[16,128,512]{2,1,0:T(8,128)S(1)}, f32[8,256,256]{2,1,0:T(8,128)S(1)}) %tuple.46, (f32[16,128,512]{2,1,0:T(8,128)}, ...), branch_computations={%region_0.0_spmd, %region_1.5_spmd} | conditional | flops 73976504 | bytes 199726944 | solution.py:591
  55.3 3.6 %release.1 = (f32[16,128,512]{2,1,0:T(8,128)}, f32[8,256,256]{2,1,0:T(8,128)}) custom-call(s32[40]{0:T(128)S(1)} %get-tuple-element.22.hits_ref, s32[3,1024]{1,0:T(4,128)S(1)} %get-tuple-element.23.spos_ref, f32[1024]{0:T(1024)S(1)} %bitcast.74, f32[16,128,512]{2,1,0:T(8,128)S(1)} %get-tuple-element.25.heated_hbm, f32[8,256,256]{2,1,0:T(8,128)S(1)} %get-tuple-element.26.phase_hbm), custom_call_target="tpu_custom_call" | custom-call | tf_op jit(solution)/shard_map/cond/branch_0_fun/release/pallas_call | solution.py:575
Async XLA Ops:
  1.3 54.0 %copy-start.9 = (s32[1024,3]{0,1:T(4,128)S(1)}, s32[1024,3]{0,1:T(4,128)}, u32[]{:S(2)}) copy-start(s32[1024,3]{0,1:T(4,128)} %param.11) | copy-start | bytes 36868
  1.3 54.0 %copy-start.10 = (s32[8,2]{0,1:T(2,128)S(1)}, s32[8,2]{0,1:T(2,128)}, u32[]{:S(2)}) copy-start(s32[8,2]{0,1:T(2,128)} %param.13) | copy-start | bytes 196

commit v3 on v2

--- a/solution.py
+++ b/solution.py
@@ -19,7 +19,9 @@
 CX, CY, CZ = 16, 128, 512
 CAP = 5
 HIT_CAP = 32
-HIT_GROUP = 4
+HIT_GROUP = 8
+LANES = 128
+STRIP_GROUP = 4
 EDGE_ROWS = 24
 MESH = pl.DeviceIdType.MESH
 F32 = jnp.float32
@@ -142,7 +144,7 @@
     return rank, jnp.sum(touched.astype(I32))
 
 
-def share_of(s, valid, spos_ref, e_ref, a, b, lane):
+def share_of(s, valid, spos_ref, e_ref, a, b, lane_z):
     px, py = local_cell(spos_ref[0, s], spos_ref[1, s], a, b)
     z = spos_ref[2, s]
     okx = (px >= 0) & (px < CX) & valid
@@ -151,7 +153,8 @@
     y0 = jnp.clip(py, 0, CY - 1)
 
     def part(x, y, ok):
-        t = thermal_distribution(e_ref[jnp.clip(x, 0, CX - 1), pl.ds(jnp.clip(y, 0, CY - 1), 1), :])
+        x, y = jnp.clip(x, 0, CX - 1), jnp.clip(y, 0, CY - 1)
+        t = thermal_distribution(e_ref[x, pl.ds(y, 1), :])
         return jnp.where(ok, t, 0.0)
 
     own = jnp.where(okx & oky, e_ref[x0, pl.ds(y0, 1), :], 0.0)
@@ -162,10 +165,9 @@
         + part(x0, py - 1, okx & (py >= 1) & (py <= CY))
         + part(x0, py + 1, okx & (py >= -1) & (py < CY - 1))
     )
-    here = lane == z
-    beside = (lane == z - 1) | (lane == z + 1)
-    value = jnp.where(here, own + DT_MACRO * (ring - 6.0 * t), 0.0) + jnp.where(beside, DT_MACRO * t, 0.0)
-    return jnp.sum(value, keepdims=True)
+    beside = (lane_z == z - 1) | (lane_z == z + 1)
+    line = jnp.where(lane_z == z, own + DT_MACRO * (ring - 6.0 * t), 0.0) + jnp.where(beside, DT_MACRO * t, 0.0)
+    return (line[:, 0:128] + line[:, 128:256]) + (line[:, 256:384] + line[:, 384:512])
 
 
 def seam_tables(nb_ref, place_ref, recv_ref, a):
@@ -199,25 +201,27 @@
     return sends, over
 
 
-def lane_sum(halves, lane):
-    first, second = halves
-    l0, l1 = pltpu.roll(first, 1, 1), pltpu.roll(second, 1, 1)
-    r0, r1 = pltpu.roll(first, 127, 1), pltpu.roll(second, 127, 1)
-    low, high = lane == 0, lane == 127
-    return (
-        jnp.where(low, 1.0, l0) + jnp.where(high, r1, r0),
-        jnp.where(low, l0, l1) + jnp.where(high, 0.0, r1),
-    )
+def along_rows(halves, lane):
+    even, odd = halves
+    axis = even.ndim - 1
+    above = jnp.where(lane == 0, 1.0, pltpu.roll(odd, 1, axis))
+    below = jnp.where(lane == LANES - 1, 0.0, pltpu.roll(even, LANES - 1, axis))
+    return above + odd, even + below
+
+
+def along_columns(c):
+    n = c.shape[0]
+    first = pltpu.roll(c[n - 1], 1, 0)[None]
+    last = pltpu.roll(c[0], 7, 0)[None]
+    return jnp.concatenate([first, c[: n - 1]], axis=0) + jnp.concatenate([c[1:], last], axis=0)
 
 
 def phase_step(halves, rates, k1, k4, lane):
-    rows = halves[0].shape[0]
-    beside = lane_sum(halves, lane)
+    beside = along_rows(halves, lane)
     out = []
     for h in range(2):
         c = halves[h]
-        around = beside[h] + (pltpu.roll(c, 1, 0) + pltpu.roll(c, rows - 1, 0))
-        out.append(c + rates[h] * (around + c * (c * (k1 - c) - k4)))
+        out.append(c + rates[h] * ((beside[h] + along_columns(c)) + c * (c * (k1 - c) - k4)))
     return tuple(out)
 
 
@@ -226,7 +230,7 @@
     heated_ref, out_ref, latent_ref, over_ref, hits_ref,
     send_v, send_ref, recv_ref, place_ref, posb, shares,
     e_ref, t_ref, p_ref, m_ref, pt, mt, ct, eb, sb, rb, stp, stm,
-    hx, hy, ty, c_out, c1, c2, sum1, lat, l1, l2, latsum, nb_t,
+    hx, hy, ty, c_out, c1, c2, sum1, lat, l1, l2, latsum, nb_t, weave, rows_v,
     load_sem, s1s, s1r, s2s, s2r, es, er, hxs, hxr, hys, hyr, l1s, l1r, l2s, l2r,
 ):
     a, b = lax.axis_index("axial"), lax.axis_index("azim")
@@ -236,50 +240,97 @@
     for peer in az + ax:
         pl.semaphore_signal(barrier, inc=1, device_id=peer, device_id_type=MESH)
 
-    load_p = pltpu.make_async_copy(phase_hbm, p_ref, load_sem.at[0])
-    load_m = pltpu.make_async_copy(mob_hbm, m_ref, load_sem.at[1])
-    load_e = pltpu.make_async_copy(e_hbm, e_ref, load_sem.at[2])
+    load_e = pltpu.make_async_copy(e_hbm, e_ref, load_sem.at[4])
     load_e.start()
-    load_p.start()
-    load_m.start()
+    loads = []
+    for k, (src, dst) in enumerate(((phase_hbm, p_ref), (mob_hbm, m_ref))):
+        for tile in range(2):
+            columns = pl.ds(tile * LANES, LANES)
+            loads.append(pltpu.make_async_copy(src.at[:, :, columns], dst.at[:, tile], load_sem.at[2 * k + tile]))
+    for load in loads:
+        load.start()
 
     lanes1 = lax.broadcasted_iota(I32, (1, 128), 1)
     alive_all = ((lanes1 // SLOTS == a) & (lanes1 % SLOTS < count_ref[0])).astype(F32)
     sends, over = seam_tables(nb_ref, place_ref, recv_ref, a)
     send_v[...] = sends
-    to_smem = pltpu.make_async_copy(send_v, send_ref, load_sem.at[3])
+    to_smem = pltpu.make_async_copy(send_v, send_ref, load_sem.at[5])
     to_smem.start()
     rank, count = rank_hits(pos_ref, posb, a, b)
     over = jnp.maximum(over, (count > HIT_CAP).astype(I32))
     hits_ref[0] = jnp.minimum(count, HIT_CAP)
-    shares[...] = jnp.zeros((NB, 128), F32)
     linear = lax.broadcasted_iota(I32, (NB, 128), 0) * 128 + lax.broadcasted_iota(I32, (NB, 128), 1)
     lane_z = lax.broadcasted_iota(I32, (1, CZ), 1)
-    load_e.wait()
 
     @pl.loop(0, HIT_CAP // HIT_GROUP)
     def _(i):
-        acc = shares[...]
         for j in range(HIT_GROUP):
             h = i * HIT_GROUP + j
-            s = jnp.clip(jnp.sum(jnp.where(rank == h.astype(F32), linear, 0)), 0, NA * NB * SLOTS - 1)
-            hits_ref[h + 1] = s
-            goal = ((s // SLOTS) % NB) * 128 + (s // (SLOTS * NB)) * SLOTS + s % SLOTS
-            value = share_of(s, h < count, spos_ref, e_ref, a, b, lane_z)
-            acc = acc + jnp.where(linear == goal, value, 0.0)
-        shares[...] = acc
-
-    for j in range(NB):
-        c_out[j, 0:1, :] = shares[j : j + 1, :]
-        c_out[j, 1:2, :] = jnp.full((1, 128), over, I32).astype(F32)
+            s = jnp.sum(jnp.where(rank == h.astype(F32), linear, 0))
+            hits_ref[h + 1] = jnp.clip(s, 0, NA * NB * SLOTS - 1)
+
+    load_e.wait()
+
+    @pl.loop(0, HIT_CAP // HIT_GROUP)
+    def _(i):
+        for j in range(HIT_GROUP):
+            h = i * HIT_GROUP + j
+            s = jnp.clip(hits_ref[h + 1], 0, NA * NB * SLOTS - 1)
+            rows_v[pl.ds(h, 1), :] = share_of(s, h < count, spos_ref, e_ref, a, b, lane_z)
+
+    values = jnp.sum(rows_v[...], axis=1, keepdims=True)
+    acc = jnp.zeros((NB, 128), F32)
+    for h in range(HIT_CAP):
+        s = hits_ref[h + 1]
+        goal = ((s // SLOTS) % NB) * 128 + (s // (SLOTS * NB)) * SLOTS + s % SLOTS
+        acc = acc + jnp.where(linear == goal, values[h : h + 1], 0.0)
+    shares[...] = acc
+
+    c_out[0:NB, :] = shares[...]
+    c_out[NB : NB + 1, :] = jnp.full((1, 128), over, I32).astype(F32)
 
     pl.semaphore_wait(barrier, len(az) + len(ax))
 
-    for i, peer in enumerate(az):
-        pltpu.make_async_remote_copy(
-            c_out.at[peer[1]], c1.at[b], s1s, s1r, device_id=peer, device_id_type=MESH
-        ).start()
-    c1[b] = c_out[b]
+    for i, peer in enumerate(ax):
+        pltpu.make_async_remote_copy(c_out, c1.at[a], s1s, s1r, device_id=peer, device_id_type=MESH).start()
+    c1[a] = c_out[...]
+
+    for load in loads:
+        load.wait()
+    to_smem.wait()
+
+    @pl.loop(0, SLOTS)
+    def _(s):
+        for h in range(2):
+            for tile in range(2):
+                rows = pl.ds(h, LANES, stride=2)
+                ph = p_ref[s, tile, rows, :].T
+                mh = m_ref[s, tile, rows, :].T * DT_PHASE
+                for i in range(4):
+                    place = pl.ds(tile * 4 + i, 32, stride=8)
+                    pt[s, h, place, :] = ph[i * 32 : i * 32 + 32]
+                    mt[s, h, place, :] = mh[i * 32 : i * 32 + 32]
+                e = 2 * s + tile
+                base = h * 12
+                if tile == 0:
+                    eb[e, base : base + 6] = ph[0:6]
+                    eb[e, base + 6 : base + 11] = mh[0:5]
+                    stp[s, tile, h, 0:2] = jnp.zeros((2, 128), F32)
+                    stp[s, tile, h, 8:24] = ph[0:16]
+                    stm[s, tile, h, 0:3] = jnp.zeros((3, 128), F32)
+                    stm[s, tile, h, 8:24] = mh[0:16]
+                else:
+                    eb[e, base : base + 6] = ph[122:128]
+                    eb[e, base + 6 : base + 11] = mh[123:128]
+                    stp[s, tile, h, 0:16] = ph[112:128]
+                    stp[s, tile, h, 22:24] = jnp.zeros((2, 128), F32)
+                    stm[s, tile, h, 0:16] = mh[112:128]
+                    stm[s, tile, h, 21:24] = jnp.zeros((3, 128), F32)
+                eb[e, base + 11 : base + 12] = jnp.zeros((1, 128), F32)
+
+    @pl.loop(0, (NA - 1) * CAP)
+    def _(n):
+        sb[n] = eb[jnp.clip(send_ref[0, n], 0, 2 * SLOTS - 1)]
 
     @pl.loop(0, CX)
     def _(x):
@@ -295,38 +346,19 @@
     y_up.start()
     y_down.start()
 
-    load_p.wait()
-    load_m.wait()
-    to_smem.wait()
-
-    @pl.loop(0, SLOTS)
-    def _(s):
-        p = p_ref[s].T
-        m = m_ref[s].T * DT_PHASE
-        for h in range(2):
-            ph, mh = p[:, h * 128 : h * 128 + 128], m[:, h * 128 : h * 128 + 128]
-            pt[s, h] = ph
-            mt[s, h] = mh
-            base = h * 12
-            eb[2 * s, base : base + 6] = ph[0:6]
-            eb[2 * s, base + 6 : base + 11] = mh[0:5]
-            eb[2 * s + 1, base : base + 6] = ph[250:256]
-            eb[2 * s + 1, base + 6 : base + 11] = mh[251:256]
-            eb[2 * s, base + 11 : base + 12] = jnp.zeros((1, 128), F32)
-            eb[2 * s + 1, base + 11 : base + 12] = jnp.zeros((1, 128), F32)
-
-    @pl.loop(0, (NA - 1) * CAP)
-    def _(n):
-        sb[n] = eb[jnp.clip(send_ref[0, n], 0, 2 * SLOTS - 1)]
-
     whole1 = pltpu.make_async_remote_copy(
-        c_out.at[pl.ds(0, NB - 1)], c1.at[pl.ds(0, NB - 1)], s1s, s1r, device_id=az[0], device_id_type=MESH
+        c1.at[pl.ds(0, NA - 1)], c1.at[pl.ds(0, NA - 1)], s1s, s1r, device_id=ax[0], device_id_type=MESH
     )
     whole1.wait_recv()
-    sum1[...] = jnp.sum(c1[...], axis=0)
-    for i, peer in enumerate(ax):
-        pltpu.make_async_remote_copy(sum1, c2.at[a], s2s, s2r, device_id=peer, device_id_type=MESH).start()
-    c2[a] = sum1[...]
+    partial = jnp.sum(c1[...], axis=0)
+    for j in range(NB):
+        sum1[j, 0:1, :] = partial[j : j + 1]
+        sum1[j, 1:2, :] = partial[NB : NB + 1]
+    for i, peer in enumerate(az):
+        pltpu.make_async_remote_copy(
+            sum1.at[peer[1]], c2.at[b], s2s, s2r, device_id=peer, device_id_type=MESH
+        ).start()
+    c2[b] = sum1[b]
 
     for i, peer in enumerate(ax):
         pltpu.make_async_remote_copy(
@@ -361,7 +393,7 @@
         plane(x, t_ref[x - 1], t_ref[x + 1])
 
     whole2 = pltpu.make_async_remote_copy(
-        c2.at[pl.ds(0, NA - 1)], c2.at[pl.ds(0, NA - 1)], s2s, s2r, device_id=ax[0], device_id_type=MESH
+        c2.at[pl.ds(0, NB - 1)], c2.at[pl.ds(0, NB - 1)], s2s, s2r, device_id=az[0], device_id_type=MESH
     )
     whole2.wait_recv()
     total = jnp.sum(c2[...], axis=0)
@@ -371,77 +403,82 @@
     def temp_of(index):
         return jnp.sum(jnp.where(lanes1 == index, temps, 0.0), axis=1, keepdims=True)
 
-    lane_full = lax.broadcasted_iota(I32, (SIDE, 128), 1)
-    row_full = lax.broadcasted_iota(I32, (SIDE, 128), 0)
-    body = (row_full >= 6) & (row_full < SIDE - 6)
+    cells = (SIDE // 8, 8, LANES)
+    lane_full = lax.broadcasted_iota(I32, cells, 2)
+    column = lax.broadcasted_iota(I32, cells, 1) * (SIDE // 8) + lax.broadcasted_iota(I32, cells, 0)
+    body = (column >= 6) & (column < SIDE - 6)
 
     @pl.loop(0, SLOTS)
     def _(s):
         tau = temp_of(a * SLOTS + s)
         nb_t[s] = jnp.broadcast_to(tau, (1, 128))
         k1, k4 = 1.5 + DRIVE_GAIN * tau, 4.5 + DRIVE_GAIN * tau
-        cur = (pt[s, 0], pt[s, 1])
+        start = (pt[s, 0].reshape(cells), pt[s, 1].reshape(cells))
+        rates = (mt[s, 0].reshape(cells), mt[s, 1].reshape(cells))
+        cur = start
         for _step in range(PHASE_STEPS):
-            cur = phase_step(cur, (mt[s, 0], mt[s, 1]), k1, k4, lane_full)
-        ct[s, 0] = cur[0]
-        ct[s, 1] = cur[1]
-        change = (cur[0] - pt[s, 0]) + (cur[1] - pt[s, 1])
-        latsum[s] = jnp.sum(jnp.where(body, change, 0.0), axis=0, keepdims=True)
+            cur = phase_step(cur, rates, k1, k4, lane_full)
+        ct[s, 0] = cur[0].reshape(SIDE, LANES)
+        ct[s, 1] = cur[1].reshape(SIDE, LANES)
+        change = (cur[0] - start[0]) + (cur[1] - start[1])
+        latsum[s] = jnp.sum(jnp.sum(jnp.where(body, change, 0.0), axis=0), axis=0, keepdims=True)
 
     whole_e = pltpu.make_async_remote_copy(sb, rb, es, er, device_id=ax[0], device_id_type=MESH)
     whole_e.wait_recv()
-    lane_strip = lax.broadcasted_iota(I32, (24, 128), 1)
-    row_strip = lax.broadcasted_iota(I32, (24, 128), 0)
-    lat[...] = jnp.zeros((1, 128), F32)
 
     @pl.loop(0, SLOTS)
     def _(s):
-        tau = nb_t[s]
-        curs, rates, ks = [], [], []
         for side in range(2):
             e = 2 * s + side
-            own_edge = place_ref[3 * e + 1]
-            near = eb[own_edge]
+            near = eb[place_ref[3 * e + 1]]
             far = rb[recv_ref[e]]
             is_far = jnp.broadcast_to(place_ref[3 * e + 2], (EDGE_ROWS, 128)) > 0
             edge = jnp.where(is_far, far, near)
-            other = temp_of(place_ref[3 * e])
             for h in range(2):
-                ph, mh = edge[h * 12 : h * 12 + 6], edge[h * 12 + 6 : h * 12 + 11]
-                if side == 0:
-                    stp[side, h, 0:2] = jnp.zeros((2, 128), F32)
-                    stp[side, h, 2:8] = ph
-                    stp[side, h, 8:24] = pt[s, h, 0:16]
-                    stm[side, h, 0:3] = jnp.zeros((3, 128), F32)
-                    stm[side, h, 3:8] = mh
-                    stm[side, h, 8:24] = mt[s, h, 0:16]
-                else:
-                    stp[side, h, 0:16] = pt[s, h, SIDE - 16 : SIDE]
-                    stp[side, h, 16:22] = ph
-                    stp[side, h, 22:24] = jnp.zeros((2, 128), F32)
-                    stm[side, h, 0:16] = mt[s, h, SIDE - 16 : SIDE]
-                    stm[side, h, 16:21] = mh
-                    stm[side, h, 21:24] = jnp.zeros((3, 128), F32)
+                first = 2 if side == 0 else 16
+                stp[s, side, h, first : first + 6] = edge[h * 12 : h * 12 + 6]
+                first = 3 if side == 0 else 16
+                stm[s, side, h, first : first + 5] = edge[h * 12 + 6 : h * 12 + 11]
+            nb_t[SLOTS + e] = jnp.broadcast_to(temp_of(place_ref[3 * e]), (1, 128))
+
+    strip = (3, 8, LANES)
+    lane_strip = lax.broadcasted_iota(I32, strip, 2)
+    row_strip = lax.broadcasted_iota(I32, strip, 1) * 3 + lax.broadcasted_iota(I32, strip, 0)
+    lat[...] = jnp.zeros((1, 128), F32)
+
+    def woven(ref, s, side, h):
+        return jnp.stack([ref[s, side, h, pl.ds(j, 8, stride=3), :] for j in range(3)], axis=0)
+
+    @pl.loop(0, SLOTS // STRIP_GROUP)
+    def _(n):
+        pairs = [(n * STRIP_GROUP + k, side) for k in range(STRIP_GROUP) for side in range(2)]
+        curs, rates, ks = [], [], []
+        for s, side in pairs:
+            curs.append((woven(stp, s, side, 0), woven(stp, s, side, 1)))
+            rates.append((woven(stm, s, side, 0), woven(stm, s, side, 1)))
             outer = row_strip < 8 if side == 0 else row_strip >= 16
-            ks.append(DRIVE_GAIN * jnp.where(outer, other, tau))
-            curs.append((stp[side, 0], stp[side, 1]))
-            rates.append((stm[side, 0], stm[side, 1]))
+            ks.append(DRIVE_GAIN * jnp.where(outer, nb_t[SLOTS + 2 * s + side][None], nb_t[s][None]))
         starts = curs
         for _step in range(PHASE_STEPS):
-            curs = [
-                phase_step(curs[side], rates[side], 1.5 + ks[side], 4.5 + ks[side], lane_strip) for side in range(2)
-            ]
-        total_s = latsum[s]
-        for side in range(2):
-            low = 8 if side == 0 else 10
-            first = 0 if side == 0 else SIDE - 6
-            for h in range(2):
-                ct[s, h, first : first + 6] = curs[side][h][low : low + 6]
-            kept = (row_strip >= low) & (row_strip < low + 6)
-            change = (curs[side][0] - starts[side][0]) + (curs[side][1] - starts[side][1])
-            total_s = total_s + jnp.sum(jnp.where(kept, change, 0.0), axis=0, keepdims=True)
-        value = jnp.sum(total_s, axis=1, keepdims=True) * (COUPLING / (SIDE * SIDE))
-        lat[...] = jnp.where(lanes1 == a * SLOTS + s, jnp.where(alive_all > 0.5, value, 0.0), lat[...])
+            curs = [phase_step(c, r, 1.5 + k, 4.5 + k, lane_strip) for c, r, k in zip(curs, rates, ks)]
+        for k in range(STRIP_GROUP):
+            s = n * STRIP_GROUP + k
+            total_s = latsum[s]
+            for side in range(2):
+                q = 2 * k + side
+                low = 8 if side == 0 else 10
+                for h in range(2):
+                    for j in range(3):
+                        stp[s, side, h, pl.ds(j, 8, stride=3), :] = curs[q][h][j]
+                    if side == 0:
+                        ct[s, h, pl.ds(0, 6, stride=8), :] = stp[s, side, h, low : low + 6]
+                    else:
+                        ct[s, h, pl.ds(26 * 8 + 7, 6, stride=8), :] = stp[s, side, h, low : low + 6]
+                kept = (row_strip >= low) & (row_strip < low + 6)
+                change = (curs[q][0] - starts[q][0]) + (curs[q][1] - starts[q][1])
+                total_s = total_s + jnp.sum(jnp.sum(jnp.where(kept, change, 0.0), axis=0), axis=0, keepdims=True)
+            value = jnp.sum(total_s, axis=1, keepdims=True) * (COUPLING / (SIDE * SIDE))
+            lat[...] = jnp.where(lanes1 == a * SLOTS + s, jnp.where(alive_all > 0.5, value, 0.0), lat[...])
 
     for i, peer in enumerate(ax):
         pltpu.make_async_remote_copy(lat, l1.at[a], l1s, l1r, device_id=peer, device_id_type=MESH).start()
@@ -465,8 +502,14 @@
     def _(s):
         alive = jnp.sum(jnp.where(lanes1 == a * SLOTS + s, alive_all, 0.0), axis=1, keepdims=True)
         for h in range(2):
-            final = jnp.where(alive > 0.5, ct[s, h], pt[s, h])
-            out_ref[s, h * 128 : h * 128 + 128, :] = final.T
+            for tile in range(2):
+                parts = []
+                for i in range(4):
+                    place = pl.ds(tile * 4 + i, 32, stride=8)
+                    parts.append(jnp.where(alive > 0.5, ct[s, h, place, :], pt[s, h, place, :]))
+                weave[tile, pl.ds(h, LANES, stride=2), :] = jnp.concatenate(parts, axis=0).T
+        for tile in range(2):
+            out_ref[s, :, tile * LANES : tile * LANES + LANES] = weave[tile]
 
     whole_l2 = pltpu.make_async_remote_copy(
         l2.at[pl.ds(0, NB - 1)], l2.at[pl.ds(0, NB - 1)], l2s, l2r, device_id=az[0], device_id_type=MESH
@@ -538,29 +581,31 @@
             VMEM((NB, 128), F32),
             VMEM((CX, CY, CZ), F32),
             VMEM((CX, CY, CZ), F32),
-            VMEM((SLOTS, SIDE, SIDE), F32),
-            VMEM((SLOTS, SIDE, SIDE), F32),
+            VMEM((SLOTS, 2, SIDE, LANES), F32),
+            VMEM((SLOTS, 2, SIDE, LANES), F32),
             VMEM((SLOTS, 2, SIDE, 128), F32),
             VMEM((SLOTS, 2, SIDE, 128), F32),
             VMEM((SLOTS, 2, SIDE, 128), F32),
             VMEM((2 * SLOTS, EDGE_ROWS, 128), F32),
             VMEM(((NA - 1) * CAP, EDGE_ROWS, 128), F32),
             VMEM(((NA - 1) * CAP, EDGE_ROWS, 128), F32),
-            VMEM((2, 2, 24, 128), F32),
-            VMEM((2, 2, 24, 128), F32),
+            VMEM((SLOTS, 2, 2, 24, 128), F32),
+            VMEM((SLOTS, 2, 2, 24, 128), F32),
             VMEM((2, CY, CZ), F32),
             VMEM((2, CX, 1, CZ), F32),
             VMEM((2, CX, 1, CZ), F32),
+            VMEM((NB + 1, 128), F32),
+            VMEM((NA, NB + 1, 128), F32),
             VMEM((NB, 2, 128), F32),
             VMEM((NB, 2, 128), F32),
-            VMEM((NA, 2, 128), F32),
-            VMEM((2, 128), F32),
             VMEM((1, 128), F32),
             VMEM((NA, 1, 128), F32),
             VMEM((NB, 1, 128), F32),
             VMEM((SLOTS, 1, 128), F32),
-            VMEM((SLOTS, 1, 128), F32),
-            DMA((4,)),
+            VMEM((3 * SLOTS, 1, 128), F32),
+            VMEM((2, SIDE, LANES), F32),
+            VMEM((HIT_CAP, LANES), F32),
+            DMA((6,)),
             DMA, DMA, DMA, DMA, DMA, DMA,
             DMA((2,)), DMA((2,)), DMA((2,)), DMA((2,)),
             DMA, DMA, DMA, DMA,

time: 59.5 us -> 48.2 us (0.81)
  Pallas kernels: 57.5 us -> 46.2 us
    pallas_call x1, Pallas kernels: 53.9 us -> 42.6 us  [shards(): pl.pallas_call(main_kernel, out_shape=(jax.ShapeDtypeStruct((CX, CY, CZ),...]
where the time goes in v3:
time: 48.2 us; the launch traced here: 48 us
  Pallas kernels  46.2 us (96%)
  between operations  1.53 us (3%)
    pallas_call x1, Pallas kernels, shards(): pl.pallas_call(main_kernel, out_shape=(jax.ShapeDtypeStruct((CX, CY, CZ),...  42.6 us
    pallas_call x1, Pallas kernels, finish(): pl.pallas_call(release_kernel, out_shape=(jax.ShapeDtypeStruct((CX, CY, C...  3.6 us

profile of v3, /device:TPU:1, one launch (start us, length us, event | category | flops | bytes accessed | tf_op | source)
XLA Modules:
  0.0 48.0 jit_solution(3545072217569524025)
XLA Ops:
  1.3 0.0 copy-start.9
  1.3 0.0 copy-start.10
  1.3 42.6 %couple.1 = (f32[16,128,512]{2,1,0:T(8,128)S(1)}, f32[8,256,256]{2,1,0:T(8,128)S(1)}, f32[8,128]{1,0:T(8,128)S(1)}, f32[1,128]{1,0:T(1,128)S(1)}, s32[40]{0:T(128)S(1)}) custom-call(s32[3,1024]{1,0:T(4,128)} %bitcast.56, s32[3,1024]{1,0:T(4,128)} %bitcast.57, s32[2,8]{1,0:T(2,128)} %bitcast.73, s32[1]{0:T(128)S(6)} %copy.52.count_ref, ...), custom_call_target="tpu_custom_call" | custom-call | tf_op jit(solution)/shard_map/couple/pallas_call | solution.py:564
  44.0 0.0 copy-done.9
  44.0 0.0 copy-done.10
  44.0 3.8 %conditional.1 = ((f32[16,128,512]{2,1,0:T(8,128)}, f32[8,256,256]{2,1,0:T(8,128)})) conditional(s32[]{:T(128)} %bitcast.31, (f32[8,128]{1,0:T(8,128)S(1)}, s32[40]{0:T(128)S(1)}, s32[3,1024]{1,0:T(4,128)S(1)}, f32[16,128,512]{2,1,0:T(8,128)S(1)}, f32[8,256,256]{2,1,0:T(8,128)S(1)}) %tuple.46, (f32[16,128,512]{2,1,0:T(8,128)}, ...), branch_computations={%region_0.0_spmd, %region_1.5_spmd} | conditional | flops 73976504 | bytes 199726944 | solution.py:636
  44.0 3.6 %release.1 = (f32[16,128,512]{2,1,0:T(8,128)}, f32[8,256,256]{2,1,0:T(8,128)}) custom-call(s32[40]{0:T(128)S(1)} %get-tuple-element.22.hits_ref, s32[3,1024]{1,0:T(4,128)S(1)} %get-tuple-element.23.spos_ref, f32[1024]{0:T(1024)S(1)} %bitcast.74, f32[16,128,512]{2,1,0:T(8,128)S(1)} %get-tuple-element.25.heated_hbm, f32[8,256,256]{2,1,0:T(8,128)S(1)} %get-tuple-element.26.phase_hbm), custom_call_target="tpu_custom_call" | custom-call | tf_op jit(solution)/shard_map/cond/branch_0_fun/release/pallas_call | solution.py:620
Async XLA Ops:
  1.3 42.7 %copy-start.9 = (s32[1024,3]{0,1:T(4,128)S(1)}, s32[1024,3]{0,1:T(4,128)}, u32[]{:S(2)}) copy-start(s32[1024,3]{0,1:T(4,128)} %param.11) | copy-start | bytes 36868
  1.3 42.7 %copy-start.10 = (s32[8,2]{0,1:T(2,128)S(1)}, s32[8,2]{0,1:T(2,128)}, u32[]{:S(2)}) copy-start(s32[8,2]{0,1:T(2,128)} %param.13) | copy-start | bytes 196

commit v4 on v3

--- a/solution.py
+++ b/solution.py
@@ -22,7 +22,7 @@
 HIT_GROUP = 8
 LANES = 128
 STRIP_GROUP = 4
-EDGE_ROWS = 24
+EDGE_ROWS = 22
 MESH = pl.DeviceIdType.MESH
 F32 = jnp.float32
 I32 = jnp.int32
@@ -311,7 +311,7 @@
                     pt[s, h, place, :] = ph[i * 32 : i * 32 + 32]
                     mt[s, h, place, :] = mh[i * 32 : i * 32 + 32]
                 e = 2 * s + tile
-                base = h * 12
+                base = h * 11
                 if tile == 0:
                     eb[e, base : base + 6] = ph[0:6]
                     eb[e, base + 6 : base + 11] = mh[0:5]
@@ -326,11 +326,13 @@
                     stp[s, tile, h, 22:24] = jnp.zeros((2, 128), F32)
                     stm[s, tile, h, 0:16] = mh[112:128]
                     stm[s, tile, h, 21:24] = jnp.zeros((3, 128), F32)
-                eb[e, base + 11 : base + 12] = jnp.zeros((1, 128), F32)
-
-    @pl.loop(0, (NA - 1) * CAP)
-    def _(n):
-        sb[n] = eb[jnp.clip(send_ref[0, n], 0, 2 * SLOTS - 1)]
+
+    for i, peer in enumerate(ax):
+        for n in range(i * CAP, (i + 1) * CAP):
+            sb[n] = eb[jnp.clip(send_ref[0, n], 0, 2 * SLOTS - 1)]
+        pltpu.make_async_remote_copy(
+            sb.at[pl.ds(i * CAP, CAP)], rb.at[pl.ds(i * CAP, CAP)], es, er, device_id=peer, device_id_type=MESH
+        ).start()
 
     @pl.loop(0, CX)
     def _(x):
@@ -359,11 +361,6 @@
             sum1.at[peer[1]], c2.at[b], s2s, s2r, device_id=peer, device_id_type=MESH
         ).start()
     c2[b] = sum1[b]
-
-    for i, peer in enumerate(ax):
-        pltpu.make_async_remote_copy(
-            sb.at[pl.ds(i * CAP, CAP)], rb.at[pl.ds(i * CAP, CAP)], es, er, device_id=peer, device_id_type=MESH
-        ).start()
 
     x_up = pltpu.make_async_remote_copy(
         t_ref.at[CX - 1], hx.at[0], hxs.at[0], hxr.at[0], device_id=up_a, device_id_type=MESH
@@ -436,9 +433,9 @@
             edge = jnp.where(is_far, far, near)
             for h in range(2):
                 first = 2 if side == 0 else 16
-                stp[s, side, h, first : first + 6] = edge[h * 12 : h * 12 + 6]
+                stp[s, side, h, first : first + 6] = edge[h * 11 : h * 11 + 6]
                 first = 3 if side == 0 else 16
-                stm[s, side, h, first : first + 5] = edge[h * 12 + 6 : h * 12 + 11]
+                stm[s, side, h, first : first + 5] = edge[h * 11 + 6 : h * 11 + 11]
             nb_t[SLOTS + e] = jnp.broadcast_to(temp_of(place_ref[3 * e]), (1, 128))
 
     strip = (3, 8, LANES)

time: 48.2 us -> 44.2 us (0.917)
  Pallas kernels: 46.2 us -> 42.2 us
    pallas_call x1, Pallas kernels: 42.6 us -> 38.6 us  [shards(): pl.pallas_call(main_kernel, out_shape=(jax.ShapeDtypeStruct((CX, CY, CZ),...]
where the time goes in v4:
time: 44.2 us; the launch traced here: 44 us
  Pallas kernels  42.2 us (95%)
  between operations  1.53 us (3%)
    pallas_call x1, Pallas kernels, shards(): pl.pallas_call(main_kernel, out_shape=(jax.ShapeDtypeStruct((CX, CY, CZ),...  38.6 us
    pallas_call x1, Pallas kernels, finish(): pl.pallas_call(release_kernel, out_shape=(jax.ShapeDtypeStruct((CX, CY, C...  3.64 us

profile of v4, /device:TPU:1, one launch (start us, length us, event | category | flops | bytes accessed | tf_op | source)
XLA Modules:
  0.0 44.0 jit_solution(16239010035855314042)
XLA Ops:
  1.3 0.0 copy-start.9
  1.3 0.0 copy-start.10
  1.3 38.6 %couple.1 = (f32[16,128,512]{2,1,0:T(8,128)S(1)}, f32[8,256,256]{2,1,0:T(8,128)S(1)}, f32[8,128]{1,0:T(8,128)S(1)}, f32[1,128]{1,0:T(1,128)S(1)}, s32[40]{0:T(128)S(1)}) custom-call(s32[3,1024]{1,0:T(4,128)} %bitcast.56, s32[3,1024]{1,0:T(4,128)} %bitcast.57, s32[2,8]{1,0:T(2,128)} %bitcast.73, s32[1]{0:T(128)S(6)} %copy.52.count_ref, ...), custom_call_target="tpu_custom_call" | custom-call | tf_op jit(solution)/shard_map/couple/pallas_call | solution.py:561
  39.9 0.0 copy-done.9
  39.9 0.0 copy-done.10
  39.9 3.9 %conditional.1 = ((f32[16,128,512]{2,1,0:T(8,128)}, f32[8,256,256]{2,1,0:T(8,128)})) conditional(s32[]{:T(128)} %bitcast.31, (f32[8,128]{1,0:T(8,128)S(1)}, s32[40]{0:T(128)S(1)}, s32[3,1024]{1,0:T(4,128)S(1)}, f32[16,128,512]{2,1,0:T(8,128)S(1)}, f32[8,256,256]{2,1,0:T(8,128)S(1)}) %tuple.46, (f32[16,128,512]{2,1,0:T(8,128)}, ...), branch_computations={%region_0.0_spmd, %region_1.5_spmd} | conditional | flops 73976504 | bytes 199726944 | solution.py:633
  39.9 3.6 %release.1 = (f32[16,128,512]{2,1,0:T(8,128)}, f32[8,256,256]{2,1,0:T(8,128)}) custom-call(s32[40]{0:T(128)S(1)} %get-tuple-element.22.hits_ref, s32[3,1024]{1,0:T(4,128)S(1)} %get-tuple-element.23.spos_ref, f32[1024]{0:T(1024)S(1)} %bitcast.74, f32[16,128,512]{2,1,0:T(8,128)S(1)} %get-tuple-element.25.heated_hbm, f32[8,256,256]{2,1,0:T(8,128)S(1)} %get-tuple-element.26.phase_hbm), custom_call_target="tpu_custom_call" | custom-call | tf_op jit(solution)/shard_map/cond/branch_0_fun/release/pallas_call | solution.py:617
Async XLA Ops:
  1.3 38.6 %copy-start.9 = (s32[1024,3]{0,1:T(4,128)S(1)}, s32[1024,3]{0,1:T(4,128)}, u32[]{:S(2)}) copy-start(s32[1024,3]{0,1:T(4,128)} %param.11) | copy-start | bytes 36868
  1.3 38.6 %copy-start.10 = (s32[8,2]{0,1:T(2,128)S(1)}, s32[8,2]{0,1:T(2,128)}, u32[]{:S(2)}) copy-start(s32[8,2]{0,1:T(2,128)} %param.13) | copy-start | bytes 196

commit v5 on v4

--- a/solution.py
+++ b/solution.py
@@ -237,7 +237,9 @@
     ax = [(lax.rem(a + i, NA), b) for i in range(1, NA)]
     az = [(a, lax.rem(b + i, NB)) for i in range(1, NB)]
     barrier = pltpu.get_barrier_semaphore()
-    for peer in az + ax:
+    hops = [min(i // 4, 4 - i // 4) + min(i % 4, 4 - i % 4) for i in range(1, NA)]
+    far_first = sorted(range(NA - 1), key=lambda k: -hops[k])
+    for peer in [ax[k] for k in far_first] + az:
         pl.semaphore_signal(barrier, inc=1, device_id=peer, device_id_type=MESH)
 
     load_e = pltpu.make_async_copy(e_hbm, e_ref, load_sem.at[4])
@@ -291,7 +293,7 @@
 
     pl.semaphore_wait(barrier, len(az) + len(ax))
 
-    for i, peer in enumerate(ax):
+    for i, peer in ((k, ax[k]) for k in far_first):
         pltpu.make_async_remote_copy(c_out, c1.at[a], s1s, s1r, device_id=peer, device_id_type=MESH).start()
     c1[a] = c_out[...]
 
@@ -327,7 +329,7 @@
                     stm[s, tile, h, 0:16] = mh[112:128]
                     stm[s, tile, h, 21:24] = jnp.zeros((3, 128), F32)
 
-    for i, peer in enumerate(ax):
+    for i, peer in ((k, ax[k]) for k in far_first):
         for n in range(i * CAP, (i + 1) * CAP):
             sb[n] = eb[jnp.clip(send_ref[0, n], 0, 2 * SLOTS - 1)]
         pltpu.make_async_remote_copy(
@@ -477,7 +479,7 @@
             value = jnp.sum(total_s, axis=1, keepdims=True) * (COUPLING / (SIDE * SIDE))
             lat[...] = jnp.where(lanes1 == a * SLOTS + s, jnp.where(alive_all > 0.5, value, 0.0), lat[...])
 
-    for i, peer in enumerate(ax):
+    for i, peer in ((k, ax[k]) for k in far_first):
         pltpu.make_async_remote_copy(lat, l1.at[a], l1s, l1r, device_id=peer, device_id_type=MESH).start()
     l1[a] = lat[...]
 

time: 44.2 us -> 44.2 us (level)
  no operation moved by 1% of the time
where the time goes in v5:
time: 44.2 us; the launch traced here: 44 us
  Pallas kernels  42.2 us (95%)
  between operations  1.53 us (3%)
    pallas_call x1, Pallas kernels, shards(): pl.pallas_call(main_kernel, out_shape=(jax.ShapeDtypeStruct((CX, CY, CZ),...  38.6 us
    pallas_call x1, Pallas kernels, finish(): pl.pallas_call(release_kernel, out_shape=(jax.ShapeDtypeStruct((CX, CY, C...  3.6 us

profile of v5, /device:TPU:1, one launch (start us, length us, event | category | flops | bytes accessed | tf_op | source)
XLA Modules:
  0.0 44.0 jit_solution(4973796834206670691)
XLA Ops:
  1.3 0.0 copy-start.9
  1.3 0.0 copy-start.10
  1.3 38.6 %couple.1 = (f32[16,128,512]{2,1,0:T(8,128)S(1)}, f32[8,256,256]{2,1,0:T(8,128)S(1)}, f32[8,128]{1,0:T(8,128)S(1)}, f32[1,128]{1,0:T(1,128)S(1)}, s32[40]{0:T(128)S(1)}) custom-call(s32[3,1024]{1,0:T(4,128)} %bitcast.56, s32[3,1024]{1,0:T(4,128)} %bitcast.57, s32[2,8]{1,0:T(2,128)} %bitcast.73, s32[1]{0:T(128)S(6)} %copy.52.count_ref, ...), custom_call_target="tpu_custom_call" | custom-call | tf_op jit(solution)/shard_map/couple/pallas_call | solution.py:563
  39.9 0.0 copy-done.9
  40.0 0.0 copy-done.10
  40.0 3.8 %conditional.1 = ((f32[16,128,512]{2,1,0:T(8,128)}, f32[8,256,256]{2,1,0:T(8,128)})) conditional(s32[]{:T(128)} %bitcast.31, (f32[8,128]{1,0:T(8,128)S(1)}, s32[40]{0:T(128)S(1)}, s32[3,1024]{1,0:T(4,128)S(1)}, f32[16,128,512]{2,1,0:T(8,128)S(1)}, f32[8,256,256]{2,1,0:T(8,128)S(1)}) %tuple.46, (f32[16,128,512]{2,1,0:T(8,128)}, ...), branch_computations={%region_0.0_spmd, %region_1.5_spmd} | conditional | flops 73976504 | bytes 199726944 | solution.py:635
  40.0 3.6 %release.1 = (f32[16,128,512]{2,1,0:T(8,128)}, f32[8,256,256]{2,1,0:T(8,128)}) custom-call(s32[40]{0:T(128)S(1)} %get-tuple-element.22.hits_ref, s32[3,1024]{1,0:T(4,128)S(1)} %get-tuple-element.23.spos_ref, f32[1024]{0:T(1024)S(1)} %bitcast.74, f32[16,128,512]{2,1,0:T(8,128)S(1)} %get-tuple-element.25.heated_hbm, f32[8,256,256]{2,1,0:T(8,128)S(1)} %get-tuple-element.26.phase_hbm), custom_call_target="tpu_custom_call" | custom-call | tf_op jit(solution)/shard_map/cond/branch_0_fun/release/pallas_call | solution.py:619
Async XLA Ops:
  1.3 38.7 %copy-start.9 = (s32[1024,3]{0,1:T(4,128)S(1)}, s32[1024,3]{0,1:T(4,128)}, u32[]{:S(2)}) copy-start(s32[1024,3]{0,1:T(4,128)} %param.11) | copy-start | bytes 36868
  1.3 38.7 %copy-start.10 = (s32[8,2]{0,1:T(2,128)S(1)}, s32[8,2]{0,1:T(2,128)}, u32[]{:S(2)}) copy-start(s32[8,2]{0,1:T(2,128)} %param.13) | copy-start | bytes 196
